TPU v7x, 256 devices: a whole 4x4x8 slice. The times are simulated.
256 devices in a mesh: space: 64 (over x, z, core), rep: 4 (over y).
Axes of the slice: x: 4, y: 4, z: 8, core: 2. Of those that a mesh axis runs over, the one named last changes fastest.
Arguments:
- feats: bfloat16 [4, 256, 512, 128], P('rep', 'space'), may hold values from -6 to 6
- w_conv: bfloat16 [27, 128, 128], replicated, may hold values from -0.109375 to 0.109375
- w_down: bfloat16 [8, 128, 128], replicated, may hold values from -0.1875 to 0.1875
- cotangent: bfloat16 [4, 256, 64, 128], P('rep', 'space'), may hold values from -6 to 6
- nbr_owner: int32 [4, 256, 6], P('rep', 'space'), may hold values from -1 to 63, as said below
- nbr_slot: int32 [4, 256, 6], P('rep', 'space'), may hold values from -1 to 3, as said below
Outputs:
- pooled: bfloat16 [4, 256, 64, 128], P('rep', 'space')
- d_feats: bfloat16 [4, 256, 512, 128], P('rep', 'space')
- d_wconv: float32 [27, 128, 128], replicated
- d_wdown: float32 [8, 128, 128], replicated
Inputs may be any that keep to these rules, and one draw needn't show every extreme that they name: `nbr_owner`: kernel maps are mutually consistent: if block b has neighbour c in direction +a then c has neighbour b in direction -a, and each block is named at most once a direction. A neighbour's owner lies within 2 space indices of the block's own. In each direction, for each other space index within 2 that exists, exactly 1 of a device's blocks has its neighbour there. `nbr_slot`: slots of listed neighbours; -1 exactly where nbr_owner is -1.
All inputs are finite; a program needn't handle non-finite values.
Results may differ from a plain program's by a relative error of at most 0.0049.
Values may be sent and summed in bfloat16 or wider, within the bound.
A program may use at most 64 MiB of HBM per device.

v0:
```python
import jax
import jax.numpy as jnp
from jax import lax
from jax.sharding import PartitionSpec as P

REACH = 2
CAP = 1


def shifted(value, axis, steps):
    count = lax.axis_size(axis)
    initial, last = (max(0, -steps), min(count, count - steps))
    return lax.ppermute(value, axis, [(source, source + steps) for source in range(initial, last)])


def deliver(pieces, owners, slot_list, position, purpose):
    block_count = pieces.shape[1]
    offsets = jnp.where(owners >= 0, owners - position, 4 * REACH + 9)
    place_ids = jnp.arange(block_count, dtype=jnp.int32)
    cap_ids = jnp.arange(CAP, dtype=jnp.int32)
    summed = jnp.zeros(pieces.shape, jnp.float32)
    for shift_by in range(-REACH, REACH + 1):
        chosen = offsets == shift_by
        if shift_by == 0:
            onehot = (
                chosen[:, None, :] & (slot_list[:, None, :] == place_ids[None, :, None])
            ).astype(pieces.dtype)
            summed = summed + jnp.einsum(
                "djb,dbk->djk",
                onehot,
                pieces,
                preferred_element_type=jnp.float32,
                precision=lax.Precision.HIGHEST,
            )
        else:
            ranking = jnp.cumsum(chosen.astype(jnp.int32), axis=1) - 1
            picked = chosen[:, None, :] & (ranking[:, None, :] == cap_ids[None, :, None])
            packed = jnp.einsum(
                "dcb,dbk->dck",
                picked.astype(pieces.dtype),
                pieces,
                preferred_element_type=jnp.float32,
                precision=lax.Precision.HIGHEST,
            ).astype(pieces.dtype)
            targets = jnp.where(
                jnp.any(picked, axis=2),
                jnp.sum(jnp.where(picked, slot_list[:, None, :], 0), axis=2),
                -1,
            )
            if purpose == "rims":
                arrived, arrived_ids = shifted((packed, targets), "space", shift_by)
            else:
                arrived, arrived_ids = shifted((packed, targets), "space", shift_by)
            onehot = (arrived_ids[:, None, :] == place_ids[None, :, None]).astype(pieces.dtype)
            summed = summed + jnp.einsum(
                "djc,dck->djk",
                onehot,
                arrived,
                preferred_element_type=jnp.float32,
                precision=lax.Precision.HIGHEST,
            )
    return summed


def extend(blocks, owners, slot_list, position):
    block_count = blocks.shape[0]
    padded = blocks
    for axis_id in range(3):
        along = axis_id + 1
        extent = padded.shape[along]
        plus_face = lax.index_in_dim(padded, extent - 1, along, keepdims=False)
        minus_face = lax.index_in_dim(padded, 0, along, keepdims=False)
        face_shape = plus_face.shape
        pieces = jnp.stack([plus_face, minus_face]).reshape(2, block_count, -1)
        pair_owner = jnp.stack([owners[:, 2 * axis_id], owners[:, 2 * axis_id + 1]])
        pair_slot = jnp.stack([slot_list[:, 2 * axis_id], slot_list[:, 2 * axis_id + 1]])
        arrived = deliver(pieces, pair_owner, pair_slot, position, "faces").astype(blocks.dtype)
        minus_halo = arrived[0].reshape(face_shape)
        plus_halo = arrived[1].reshape(face_shape)
        padded = jnp.concatenate(
            [jnp.expand_dims(minus_halo, along), padded, jnp.expand_dims(plus_halo, along)],
            axis=along,
        )
    return padded


def return_rims(grad_padded, owners, slot_list, position):
    block_count = grad_padded.shape[0]
    current = grad_padded
    for axis_id in (2, 1, 0):
        along = axis_id + 1
        extent = current.shape[along]
        minus_rim = lax.index_in_dim(current, 0, along, keepdims=False)
        plus_rim = lax.index_in_dim(current, extent - 1, along, keepdims=False)
        rim_shape = minus_rim.shape
        pieces = jnp.stack([minus_rim, plus_rim]).reshape(2, block_count, -1)
        pair_owner = jnp.stack([owners[:, 2 * axis_id + 1], owners[:, 2 * axis_id]])
        pair_slot = jnp.stack([slot_list[:, 2 * axis_id + 1], slot_list[:, 2 * axis_id]])
        arrived = deliver(pieces, pair_owner, pair_slot, position, "rims")
        interior = lax.slice_in_dim(current, 1, extent - 1, axis=along)
        lead = (slice(None),) * along
        interior = interior.at[lead + (extent - 3,)].add(arrived[0].reshape(rim_shape))
        interior = interior.at[lead + (0,)].add(arrived[1].reshape(rim_shape))
        current = interior
    return current


def convolve(padded, weights):
    width = padded.shape[-1]
    summed = jnp.zeros((padded.shape[0] * 512, width), jnp.float32)
    for tap_id in range(27):
        start_x, start_y, start_z = (tap_id // 9, tap_id // 3 % 3, tap_id % 3)
        window = padded[
            :, start_x : start_x + 8, start_y : start_y + 8, start_z : start_z + 8, :
        ].reshape(-1, width)
        summed = summed + jnp.dot(window, weights[tap_id], preferred_element_type=jnp.float32)
    return summed


def per_device(feats, w_conv, w_down, cotangent, nbr_owner, nbr_slot):
    block_count = feats.shape[1]
    width = feats.shape[3]
    position = lax.axis_index("space")
    owners = nbr_owner[0]
    slot_list = nbr_slot[0]
    blocks = feats[0].reshape(block_count, 8, 8, 8, width)
    padded = extend(blocks, owners, slot_list, position)
    pre_act = convolve(padded, w_conv)
    hidden = jax.nn.silu(pre_act).astype(jnp.bfloat16)
    hidden_sub = hidden.reshape(block_count, 4, 2, 4, 2, 4, 2, width)
    down_five = w_down.reshape(2, 2, 2, width, width)
    pooled = jnp.einsum(
        "bxiyjzkc,ijkcd->bxyzd", hidden_sub, down_five, preferred_element_type=jnp.float32
    )
    pooled = pooled.reshape(1, block_count, 64, width).astype(jnp.bfloat16)
    grad_out = cotangent[0].reshape(block_count, 4, 4, 4, width)
    grad_down = jnp.einsum(
        "bxiyjzkc,bxyzd->ijkcd", hidden_sub, grad_out, preferred_element_type=jnp.float32
    ).reshape(8, width, width)
    grad_hidden = jnp.einsum(
        "bxyzd,ijkcd->bxiyjzkc", grad_out, down_five, preferred_element_type=jnp.float32
    ).reshape(-1, width)
    sigmoid = jax.nn.sigmoid(pre_act)
    grad_pre = (grad_hidden * sigmoid * (1.0 + pre_act * (1.0 - sigmoid))).astype(jnp.bfloat16)
    grad_padded = jnp.zeros((block_count, 10, 10, 10, width), jnp.float32)
    grad_list = []
    for tap_id in range(27):
        start_x, start_y, start_z = (tap_id // 9, tap_id // 3 % 3, tap_id % 3)
        window = padded[
            :, start_x : start_x + 8, start_y : start_y + 8, start_z : start_z + 8, :
        ].reshape(-1, width)
        grad_list.append(
            jnp.einsum("rc,rd->cd", window, grad_pre, preferred_element_type=jnp.float32)
        )
        contrib = jnp.einsum(
            "rd,cd->rc", grad_pre, w_conv[tap_id], preferred_element_type=jnp.float32
        ).reshape(block_count, 8, 8, 8, width)
        grad_padded = grad_padded.at[
            :, start_x : start_x + 8, start_y : start_y + 8, start_z : start_z + 8, :
        ].add(contrib)
    grad_conv = jnp.stack(grad_list)
    d_blocks = return_rims(grad_padded, owners, slot_list, position)
    d_feats = d_blocks.reshape(1, block_count, 512, width).astype(jnp.bfloat16)
    grad_conv, grad_down = lax.psum((grad_conv, grad_down), ("space", "rep"))
    norm_factor = (
        1.0 / float(lax.axis_size("rep") * lax.axis_size("space") * block_count * 512) ** 0.5
    )
    return (pooled, d_feats, grad_conv * norm_factor, grad_down * norm_factor)


def solution(mesh):
    placed = (
        P("rep", "space", None, None),
        P(),
        P(),
        P("rep", "space", None, None),
        P("rep", "space", None),
        P("rep", "space", None),
    )
    return jax.shard_map(
        per_device,
        mesh=mesh,
        in_specs=placed,
        out_specs=(P("rep", "space", None, None), P("rep", "space", None, None), P(), P()),
        check_vma=False,
    )
```

profile of v0, /device:TPU:1, one launch (start us, length us, event | category | flops | bytes accessed | tf_op | source)
XLA Modules:
  0.0 798.8 jit_solution(16908760964093154776)
XLA Ops:
  11.3 4.4 collective-permute-start.8
  16.1 2.9 collective-permute-start.4
  19.0 3.4 collective-permute-start.6
  25.1 4.2 collective-permute-start.9
  42.5 3.6 collective-permute-start.7
  47.6 5.4 collective-permute-start.15
  55.7 2.9 collective-permute-done.11
  62.9 5.1 collective-permute-done.1
  68.0 4.6 collective-permute-start.22
  73.3 3.5 collective-permute-start.18
  77.4 4.4 collective-permute-done.18
  86.7 4.0 collective-permute-done
  90.6 3.9 collective-permute-start.30
  95.2 3.8 collective-permute-start.26
  99.7 3.4 collective-permute-done.26
  105.0 3.9 collective-permute-done.24
  108.9 2.8 collective-permute-start.28
  112.5 3.9 collective-permute-start.38
  117.1 3.1 collective-permute-start.34
  120.9 2.6 collective-permute-done.34
  125.4 3.6 collective-permute-done.32
  129.0 2.8 collective-permute-start.36
  132.6 4.8 collective-permute-start.46
  141.2 3.6 collective-permute-done.42
  146.7 3.6 collective-permute-done.40
  150.3 2.8 collective-permute-start.44
  157.9 4.4 collective-permute-start.14
  164.2 5.8 collective-permute-start.16
  180.1 3.6 collective-permute-start.21
  187.6 6.6 collective-permute-start.23
  241.3 7.9 scatter-add.111
  251.0 7.9 scatter-add.114
  263.4 7.9 scatter-add.116
  271.3 3.8 convolution_add_fusion.47
  275.1 9.8 %scatter-add.119 = f32[4,10,10,10,128]{4,3,2,1,0:T(8,128)} dynamic-update-slice(f32[4,10,10,10,128]{4,3,2,1,0:T(8,128)} %scatter-add.116, f32[4,8,8,8,128]{4,3,2,1,0:T(8,128)S(1)} %convolution_add_fusion.47, s32[]{:T(128)} %constant.1100.clone.1, s32[]{:T(128)} %bitcast.164, s32[]{:T(128)} %bitcast.165, s32[]{:T(128)} %bitcast.166, s32[]{:T(128)} %constant.1100.clone.1) | dynamic-update-slice | bytes 2097156 | tf_op jit(solution)/shard_map/scatter-add | solution.py:160
  284.9 2.6 fusion.6
  289.4 7.9 scatter-add.121
  299.1 7.9 scatter-add.124
  311.5 7.9 scatter-add.126
  321.2 7.9 scatter-add.129
  333.5 8.1 %scatter-add.131 = f32[4,10,10,10,128]{4,3,2,1,0:T(8,128)} dynamic-update-slice(f32[4,10,10,10,128]{4,3,2,1,0:T(8,128)} %fusion.4, f32[4,8,8,8,128]{4,3,2,1,0:T(8,128)S(1)} %convolution_add_fusion.39, s32[]{:T(128)} %constant.1100.clone.1, s32[]{:T(128)} %constant.1107.clone.1, s32[]{:T(128)} %constant.1107.clone.1, s32[]{:T(128)} %constant.1107.clone.1, s32[]{:T(128)} %constant.1100.clone.1) | dynamic-update-slice | bytes 2097156 | tf_op jit(solution)/shard_map/scatter-add | solution.py:160
  343.5 7.9 scatter-add.134
  351.4 2.6 fusion.3
  355.9 7.9 scatter-add.136
  365.6 7.9 scatter-add.139
  377.9 7.9 scatter-add.141
  387.7 7.9 scatter-add.144
  395.6 2.6 fusion.1
  400.0 7.9 scatter-add.146
  409.8 7.9 scatter-add.149
  417.7 2.6 fusion
  422.2 7.9 scatter-add.151
  431.9 7.9 scatter-add.154
  439.8 3.0 slice_reduce_fusion
  448.2 5.5 collective-permute-start.29
  454.3 5.4 collective-permute-start.31
  465.6 10.8 %scatter-add.155 = f32[4,10,10,8,128]{4,3,2,1,0:T(8,128)S(1)} dynamic-update-slice(f32[4,10,10,8,128]{4,3,2,1,0:T(8,128)S(1)} %slice.1966, f32[4,10,10,1,128]{4,3,2,1,0:T(1,128)S(1)} %slice_add_fusion.1, s32[]{:T(128)} %constant.1100.clone.1, s32[]{:T(128)} %constant.1100.clone.1, s32[]{:T(128)} %constant.1100.clone.1, s32[]{:T(128)} %constant.1111.clone.1, s32[]{:T(128)} %constant.1100.clone.1) | dynamic-update-slice | bytes 409604 | tf_op jit(solution)/shard_map/scatter-add | solution.py:102
  476.5 10.8 %scatter-add.156 = f32[4,10,10,8,128]{4,3,2,1,0:T(8,128)S(1)} dynamic-update-slice(f32[4,10,10,8,128]{4,3,2,1,0:T(8,128)S(1)} %scatter-add.155, f32[4,10,10,1,128]{4,3,2,1,0:T(1,128)S(1)} %slice_add_fusion, s32[]{:T(128)} %constant.1100.clone.1, s32[]{:T(128)} %constant.1100.clone.1, s32[]{:T(128)} %constant.1100.clone.1, s32[]{:T(128)} %constant.1100.clone.1, s32[]{:T(128)} %constant.1100.clone.1) | dynamic-update-slice | bytes 409604 | tf_op jit(solution)/shard_map/scatter-add | solution.py:103
  496.0 5.4 collective-permute-start.37
  502.5 4.9 collective-permute-start.39
  517.8 5.3 collective-permute-start.45
  523.6 5.5 collective-permute-start.47
  531.9 255.8 %all-reduce.4.cloned.1.call-done = (f32[27,128,128]{2,1,0:T(8,128)}, f32[8,128,128]{2,1,0:T(8,128)}) async-done(((f32[27,128,128]{2,1,0:T(8,128)}, f32[8,128,128]{2,1,0:T(8,128)}), (f32[27,128,128]{2,1,0:T(8,128)}, f32[8,128,128]{2,1,0:T(8,128)})) %all-reduce.4.cloned.1.call-update) | async-done | bytes 2293776 | tf_op jit(solution)/shard_map/psum | solution.py:164
  787.7 3.0 broadcast_multiply_fusion
  (464 shorter events, 190.6 us)
Async XLA Ops:
  7.2 29.4 %copy-start = (bf16[8,128,128]{2,1,0:T(8,128)(2,1)S(1)}, bf16[8,128,128]{2,1,0:T(8,128)(2,1)}, u32[]{:S(2)}) copy-start(bf16[8,128,128]{2,1,0:T(8,128)(2,1)} %param.74) | copy-start | bytes 786436
  7.2 29.4 %copy-start.18 = (bf16[1,4,64,128]{3,2,1,0:T(8,128)(2,1)S(1)}, bf16[1,4,64,128]{3,2,1,0:T(8,128)(2,1)}, u32[]{:S(2)}) copy-start(bf16[1,4,64,128]{3,2,1,0:T(8,128)(2,1)} %param.75) | copy-start | bytes 196612
  7.2 780.5 %all-reduce.4.cloned.1.call-start = ((), (), s32[]{:S(2)}) async-start(), calls=%async_computation | async-start | bytes 4587520 | tf_op jit(solution)/shard_map/psum | solution.py:164
  11.3 29.3 %collective-permute-start.8 = (s32[2,1]{0,1:T(1,128)S(1)}, s32[2,1]{0,1:T(1,128)S(1)}, u32[]{:S(2)}, u32[]{:S(2)}) collective-permute-start(s32[2,1]{0,1:T(1,128)S(1)} %select_bitcast_fusion.18), channel_id=1, source_target_pairs={{0,8},{4,12},{8,16},{12,20},{16,24},{20,28},{24,32},{28,36},{32,40... | collective-permute-start | bytes 32 | tf_op jit(solution)/shard_map/ppermute | solution.py:13
  16.1 26.4 %collective-permute-start.4 = (s32[2,1]{0,1:T(1,128)S(1)}, s32[2,1]{0,1:T(1,128)S(1)}, u32[]{:S(2)}, u32[]{:S(2)}) collective-permute-start(s32[2,1]{0,1:T(1,128)S(1)} %select_bitcast_fusion.20), channel_id=1, source_target_pairs={{4,0},{8,4},{12,8},{16,12},{20,16},{24,20},{28,24},{32,28},{36,32}... | collective-permute-start | bytes 32 | tf_op jit(solution)/shard_map/ppermute | solution.py:13
  19.0 27.3 %collective-permute-start.6 = (s32[2,1]{0,1:T(1,128)S(1)}, s32[2,1]{0,1:T(1,128)S(1)}, u32[]{:S(2)}, u32[]{:S(2)}) collective-permute-start(s32[2,1]{0,1:T(1,128)S(1)} %select_bitcast_fusion.19), channel_id=1, source_target_pairs={{0,4},{4,8},{8,12},{12,16},{16,20},{20,24},{24,28},{28,32},{32,36}... | collective-permute-start | bytes 32 | tf_op jit(solution)/shard_map/ppermute | solution.py:13
  22.5 25.2 %collective-permute-start.2 = (s32[2,1]{0,1:T(1,128)S(1)}, s32[2,1]{0,1:T(1,128)S(1)}, u32[]{:S(2)}, u32[]{:S(2)}) collective-permute-start(s32[2,1]{0,1:T(1,128)S(1)} %select_bitcast_fusion.21), channel_id=1, source_target_pairs={{8,0},{12,4},{16,8},{20,12},{24,16},{28,20},{32,24},{36,28},{40,32... | collective-permute-start | bytes 32 | tf_op jit(solution)/shard_map/ppermute | solution.py:13
  25.1 129.5 %collective-permute-start.9 = (bf16[2,1,8192]{2,0,1:T(2,128)(2,1)S(1)}, bf16[2,1,8192]{2,0,1:T(2,128)(2,1)S(1)}, u32[]{:S(2)}, u32[]{:S(2)}) collective-permute-start(bf16[2,1,8192]{2,0,1:T(2,128)(2,1)S(1)} %copy.239), channel_id=1, source_target_pairs={{0,8},{4,12},{8,16},{12,20},{16,24},{20,28},{24,32},{28,36},{32,40... | collective-permute-start | bytes 98312 | tf_op jit(solution)/shard_map/ppermute | solution.py:13
  37.0 118.1 %copy-start.2 = (bf16[1,4,512,128]{3,2,1,0:T(8,128)(2,1)S(1)}, bf16[1,4,512,128]{3,2,1,0:T(8,128)(2,1)}, u32[]{:S(2)}) copy-start(bf16[1,4,512,128]{3,2,1,0:T(8,128)(2,1)} %param.72) | copy-start | bytes 1572868
  40.5 114.0 %collective-permute-start.5 = (bf16[2,1,8192]{2,0,1:T(2,128)(2,1)S(1)}, bf16[2,1,8192]{2,0,1:T(2,128)(2,1)S(1)}, u32[]{:S(2)}, u32[]{:S(2)}) collective-permute-start(bf16[2,1,8192]{2,0,1:T(2,128)(2,1)S(1)} %copy.237), channel_id=1, source_target_pairs={{4,0},{8,4},{12,8},{16,12},{20,16},{24,20},{28,24},{32,28},{36,32}... | collective-permute-start | bytes 98312 | tf_op jit(solution)/shard_map/ppermute | solution.py:13
  42.5 112.1 %collective-permute-start.7 = (bf16[2,1,8192]{2,0,1:T(2,128)(2,1)S(1)}, bf16[2,1,8192]{2,0,1:T(2,128)(2,1)S(1)}, u32[]{:S(2)}, u32[]{:S(2)}) collective-permute-start(bf16[2,1,8192]{2,0,1:T(2,128)(2,1)S(1)} %copy.238), channel_id=1, source_target_pairs={{0,4},{4,8},{8,12},{12,16},{16,20},{20,24},{24,28},{28,32},{32,36}... | collective-permute-start | bytes 98312 | tf_op jit(solution)/shard_map/ppermute | solution.py:13
  46.3 108.4 %collective-permute-start.3 = (bf16[2,1,8192]{2,0,1:T(2,128)(2,1)S(1)}, bf16[2,1,8192]{2,0,1:T(2,128)(2,1)S(1)}, u32[]{:S(2)}, u32[]{:S(2)}) collective-permute-start(bf16[2,1,8192]{2,0,1:T(2,128)(2,1)S(1)} %copy.236), channel_id=1, source_target_pairs={{8,0},{12,4},{16,8},{20,12},{24,16},{28,20},{32,24},{36,28},{40,32... | collective-permute-start | bytes 98312 | tf_op jit(solution)/shard_map/ppermute | solution.py:13
  47.6 6.1 collective-permute-start.15
  53.7 4.8 collective-permute-start.11
  58.6 3.0 collective-permute-start.13
  61.6 6.5 collective-permute-start.1
  68.0 5.3 collective-permute-start.22
  73.3 8.5 %collective-permute-start.18 = (s32[2,1]{0,1:T(1,128)S(1)}, s32[2,1]{0,1:T(1,128)S(1)}, u32[]{:S(2)}, u32[]{:S(2)}) collective-permute-start(s32[2,1]{0,1:T(1,128)S(1)} %select_bitcast_fusion.14), channel_id=1, source_target_pairs={{4,0},{8,4},{12,8},{16,12},{20,16},{24,20},{28,24},{32,28},{36,32}... | collective-permute-start | bytes 32 | tf_op jit(solution)/shard_map/ppermute | solution.py:13
  81.8 3.0 collective-permute-start.20
  84.8 5.9 collective-permute-start
  90.6 4.6 collective-permute-start.30
  95.2 7.9 collective-permute-start.26
  103.1 5.9 collective-permute-start.24
  108.9 3.5 collective-permute-start.28
  112.5 4.6 collective-permute-start.38
  117.1 6.5 collective-permute-start.34
  123.5 5.5 collective-permute-start.32
  129.0 3.5 collective-permute-start.36
  132.6 5.5 collective-permute-start.46
  138.1 6.7 collective-permute-start.42
  144.8 5.5 collective-permute-start.40
  150.3 3.5 collective-permute-start.44
  155.7 14.3 %collective-permute-start.12 = (bf16[2,1,10240]{2,0,1:T(2,128)(2,1)S(1)}, bf16[2,1,10240]{2,0,1:T(2,128)(2,1)S(1)}, u32[]{:S(2)}, u32[]{:S(2)}) collective-permute-start(bf16[2,1,10240]{2,0,1:T(2,128)(2,1)S(1)} %copy.233), channel_id=1, source_target_pairs={{4,0},{8,4},{12,8},{16,12},{20,16},{24,20},{28,24},{32,28},{36,32}... | collective-permute-start | bytes 122888 | tf_op jit(solution)/shard_map/ppermute | solution.py:13
  157.9 12.2 %collective-permute-start.14 = (bf16[2,1,10240]{2,0,1:T(2,128)(2,1)S(1)}, bf16[2,1,10240]{2,0,1:T(2,128)(2,1)S(1)}, u32[]{:S(2)}, u32[]{:S(2)}) collective-permute-start(bf16[2,1,10240]{2,0,1:T(2,128)(2,1)S(1)} %copy.234), channel_id=1, source_target_pairs={{0,4},{4,8},{8,12},{12,16},{16,20},{20,24},{24,28},{28,32},{32,36}... | collective-permute-start | bytes 122888 | tf_op jit(solution)/shard_map/ppermute | solution.py:13
  162.6 7.5 collective-permute-start.10
  164.2 6.9 collective-permute-start.16
  176.9 18.7 %collective-permute-start.19 = (bf16[2,1,12800]{2,0,1:T(2,128)(2,1)S(1)}, bf16[2,1,12800]{2,0,1:T(2,128)(2,1)S(1)}, u32[]{:S(2)}, u32[]{:S(2)}) collective-permute-start(bf16[2,1,12800]{2,0,1:T(2,128)(2,1)S(1)} %copy.229), channel_id=1, source_target_pairs={{4,0},{8,4},{12,8},{16,12},{20,16},{24,20},{28,24},{32,28},{36,32}... | collective-permute-start | bytes 153608 | tf_op jit(solution)/shard_map/ppermute | solution.py:13
  180.1 15.6 %collective-permute-start.21 = (bf16[2,1,12800]{2,0,1:T(2,128)(2,1)S(1)}, bf16[2,1,12800]{2,0,1:T(2,128)(2,1)S(1)}, u32[]{:S(2)}, u32[]{:S(2)}) collective-permute-start(bf16[2,1,12800]{2,0,1:T(2,128)(2,1)S(1)} %copy.230), channel_id=1, source_target_pairs={{0,4},{4,8},{8,12},{12,16},{16,20},{20,24},{24,28},{28,32},{32,36}... | collective-permute-start | bytes 153608 | tf_op jit(solution)/shard_map/ppermute | solution.py:13
  185.0 10.7 %collective-permute-start.17 = (bf16[2,1,12800]{2,0,1:T(2,128)(2,1)S(1)}, bf16[2,1,12800]{2,0,1:T(2,128)(2,1)S(1)}, u32[]{:S(2)}, u32[]{:S(2)}) collective-permute-start(bf16[2,1,12800]{2,0,1:T(2,128)(2,1)S(1)} %copy.228), channel_id=1, source_target_pairs={{8,0},{12,4},{16,8},{20,12},{24,16},{28,20},{32,24},{36,28},{40,32... | collective-permute-start | bytes 153608 | tf_op jit(solution)/shard_map/ppermute | solution.py:13
  187.6 8.2 %collective-permute-start.23 = (bf16[2,1,12800]{2,0,1:T(2,128)(2,1)S(1)}, bf16[2,1,12800]{2,0,1:T(2,128)(2,1)S(1)}, u32[]{:S(2)}, u32[]{:S(2)}) collective-permute-start(bf16[2,1,12800]{2,0,1:T(2,128)(2,1)S(1)} %copy.231), channel_id=1, source_target_pairs={{0,8},{4,12},{8,16},{12,20},{16,24},{20,28},{24,32},{28,36},{32,40... | collective-permute-start | bytes 153608 | tf_op jit(solution)/shard_map/ppermute | solution.py:13
  195.7 16.4 %copy-start.5 = (bf16[4,8,8,8,128]{4,3,2,1,0:T(8,128)(2,1)}, bf16[4,8,8,8,128]{4,3,2,1,0:T(8,128)(2,1)S(1)}, u32[]{:S(2)}) copy-start(bf16[4,8,8,8,128]{4,3,2,1,0:T(8,128)(2,1)S(1)} %get-tuple-element.519) | copy-start | bytes 1572868
  200.9 11.4 %copy-start.13 = (bf16[4,8,8,8,128]{4,3,2,1,0:T(8,128)(2,1)}, bf16[4,8,8,8,128]{4,3,2,1,0:T(8,128)(2,1)S(1)}, u32[]{:S(2)}) copy-start(bf16[4,8,8,8,128]{4,3,2,1,0:T(8,128)(2,1)S(1)} %get-tuple-element.495) | copy-start | bytes 1572868
  213.9 24.4 %copy-start.15 = (bf16[2048,128]{1,0:T(8,128)(2,1)}, bf16[2048,128]{1,0:T(8,128)(2,1)S(1)}, u32[]{:S(2)}) copy-start(bf16[2048,128]{1,0:T(8,128)(2,1)S(1)} %get-tuple-element.516) | copy-start | bytes 1572868
  443.6 18.6 %collective-permute-start.25 = (f32[2,1,12800]{2,0,1:T(2,128)S(1)}, f32[2,1,12800]{2,0,1:T(2,128)S(1)}, u32[]{:S(2)}, u32[]{:S(2)}) collective-permute-start(f32[2,1,12800]{2,0,1:T(2,128)S(1)} %copy.96), channel_id=1, source_target_pairs={{8,0},{12,4},{16,8},{20,12},{24,16},{28,20},{32,24},{36,28},{40,32... | collective-permute-start | bytes 307208 | tf_op jit(solution)/shard_map/ppermute | solution.py:13
  445.4 16.7 %collective-permute-start.27 = (f32[2,1,12800]{2,0,1:T(2,128)S(1)}, f32[2,1,12800]{2,0,1:T(2,128)S(1)}, u32[]{:S(2)}, u32[]{:S(2)}) collective-permute-start(f32[2,1,12800]{2,0,1:T(2,128)S(1)} %copy.98), channel_id=1, source_target_pairs={{4,0},{8,4},{12,8},{16,12},{20,16},{24,20},{28,24},{32,28},{36,32}... | collective-permute-start | bytes 307208 | tf_op jit(solution)/shard_map/ppermute | solution.py:13
  448.2 14.0 %collective-permute-start.29 = (f32[2,1,12800]{2,0,1:T(2,128)S(1)}, f32[2,1,12800]{2,0,1:T(2,128)S(1)}, u32[]{:S(2)}, u32[]{:S(2)}) collective-permute-start(f32[2,1,12800]{2,0,1:T(2,128)S(1)} %copy.100), channel_id=1, source_target_pairs={{0,4},{4,8},{8,12},{12,16},{16,20},{20,24},{24,28},{28,32},{32,36}... | collective-permute-start | bytes 307208 | tf_op jit(solution)/shard_map/ppermute | solution.py:13
  454.3 7.9 collective-permute-start.31
  487.3 20.0 %copy-start.14 = (bf16[4,8,8,8,128]{4,3,2,1,0:T(8,128)(2,1)S(1)}, bf16[4,8,8,8,128]{4,3,2,1,0:T(8,128)(2,1)}, u32[]{:S(2)}) copy-start(bf16[4,8,8,8,128]{4,3,2,1,0:T(8,128)(2,1)} %copy-done.13) | copy-start | bytes 1572868
  491.2 18.7 %collective-permute-start.33 = (f32[2,1,10240]{2,0,1:T(2,128)S(1)}, f32[2,1,10240]{2,0,1:T(2,128)}, u32[]{:S(2)}, u32[]{:S(2)}) collective-permute-start(f32[2,1,10240]{2,0,1:T(2,128)S(1)} %copy.104), channel_id=1, source_target_pairs={{8,0},{12,4},{16,8},{20,12},{24,16},{28,20},{32,24},{36,28},{40,32... | collective-permute-start | bytes 245768 | tf_op jit(solution)/shard_map/ppermute | solution.py:13
  492.9 17.0 %collective-permute-start.35 = (f32[2,1,10240]{2,0,1:T(2,128)S(1)}, f32[2,1,10240]{2,0,1:T(2,128)}, u32[]{:S(2)}, u32[]{:S(2)}) collective-permute-start(f32[2,1,10240]{2,0,1:T(2,128)S(1)} %copy.106), channel_id=1, source_target_pairs={{4,0},{8,4},{12,8},{16,12},{20,16},{24,20},{28,24},{32,28},{36,32}... | collective-permute-start | bytes 245768 | tf_op jit(solution)/shard_map/ppermute | solution.py:13
  496.0 13.9 %collective-permute-start.37 = (f32[2,1,10240]{2,0,1:T(2,128)}, f32[2,1,10240]{2,0,1:T(2,128)}, u32[]{:S(2)}, u32[]{:S(2)}) collective-permute-start(f32[2,1,10240]{2,0,1:T(2,128)} %copy.108), channel_id=1, source_target_pairs={{0,4},{4,8},{8,12},{12,16},{16,20},{20,24},{24,28},{28,32},{32,36}... | collective-permute-start | bytes 245768 | tf_op jit(solution)/shard_map/ppermute | solution.py:13
  502.5 7.4 collective-permute-start.39
  513.1 16.9 %copy-start.4 = (f32[4,10,8,8,128]{4,3,2,1,0:T(8,128)S(1)}, f32[4,10,8,8,128]{4,3,2,1,0:T(8,128)}, u32[]{:S(2)}) copy-start(f32[4,10,8,8,128]{4,3,2,1,0:T(8,128)} %copy-done.3) | copy-start | bytes 3932164
  513.7 16.4 %collective-permute-start.41 = (f32[2,1,8192]{2,0,1:T(2,128)S(1)}, f32[2,1,8192]{2,0,1:T(2,128)S(1)}, u32[]{:S(2)}, u32[]{:S(2)}) collective-permute-start(f32[2,1,8192]{2,0,1:T(2,128)S(1)} %copy.112), channel_id=1, source_target_pairs={{8,0},{12,4},{16,8},{20,12},{24,16},{28,20},{32,24},{36,28},{40,32... | collective-permute-start | bytes 196616 | tf_op jit(solution)/shard_map/ppermute | solution.py:13
  515.4 14.7 %collective-permute-start.43 = (f32[2,1,8192]{2,0,1:T(2,128)S(1)}, f32[2,1,8192]{2,0,1:T(2,128)S(1)}, u32[]{:S(2)}, u32[]{:S(2)}) collective-permute-start(f32[2,1,8192]{2,0,1:T(2,128)S(1)} %copy.114), channel_id=1, source_target_pairs={{4,0},{8,4},{12,8},{16,12},{20,16},{24,20},{28,24},{32,28},{36,32}... | collective-permute-start | bytes 196616 | tf_op jit(solution)/shard_map/ppermute | solution.py:13
  517.7 12.7 %copy-start.20 = (s32[2,4]{1,0:T(2,128)S(1)}, s32[2,4]{1,0:T(2,128)}, u32[]{:S(2)}) copy-start(s32[2,4]{1,0:T(2,128)} %get-tuple-element.545) | copy-start | bytes 100
  517.7 12.7 %copy-start.22 = (pred[2,4]{1,0:T(4,128)(4,1)S(1)}, pred[2,4]{1,0:T(4,128)(4,1)}, u32[]{:S(2)}) copy-start(pred[2,4]{1,0:T(4,128)(4,1)} %get-tuple-element.600) | copy-start | bytes 28
  517.7 12.7 %copy-start.26 = (f32[2,4]{1,0:T(2,128)S(1)}, f32[2,4]{1,0:T(2,128)}, u32[]{:S(2)}) copy-start(f32[2,4]{1,0:T(2,128)} %compare_convert_fusion) | copy-start | bytes 100
  517.7 12.7 %copy-start.27 = (f32[2,4]{1,0:T(2,128)S(1)}, f32[2,4]{1,0:T(2,128)}, u32[]{:S(2)}) copy-start(f32[2,4]{1,0:T(2,128)} %compare_convert_fusion.2) | copy-start | bytes 100
  517.7 12.7 %copy-start.28 = (f32[2,4]{1,0:T(2,128)S(1)}, f32[2,4]{1,0:T(2,128)}, u32[]{:S(2)}) copy-start(f32[2,4]{1,0:T(2,128)} %compare_convert_fusion.3) | copy-start | bytes 100
  517.7 12.7 %copy-start.29 = (f32[2,4]{1,0:T(2,128)S(1)}, f32[2,4]{1,0:T(2,128)}, u32[]{:S(2)}) copy-start(f32[2,4]{1,0:T(2,128)} %compare_convert_fusion.1) | copy-start | bytes 100
  517.8 12.3 %collective-permute-start.45 = (f32[2,1,8192]{2,0,1:T(2,128)S(1)}, f32[2,1,8192]{2,0,1:T(2,128)S(1)}, u32[]{:S(2)}, u32[]{:S(2)}) collective-permute-start(f32[2,1,8192]{2,0,1:T(2,128)S(1)} %copy.116), channel_id=1, source_target_pairs={{0,4},{4,8},{8,12},{12,16},{16,20},{20,24},{24,28},{28,32},{32,36}... | collective-permute-start | bytes 196616 | tf_op jit(solution)/shard_map/ppermute | solution.py:13
  523.6 6.8 collective-permute-start.47
  787.7 3.0 copy-start.17
  (27 other events, 30.1 us)
Sparse Core Ops, SparseCore 0:
  509.8 277.8 all-reduce.3
where the time goes:
time: 815 us; the launch traced here: 799 us
  waiting for transfers between devices  297 us (36%)
  local copies, waits for them, and re-layouts  199 us (24%)
  starting transfers between devices  148 us (18%)
  matrix products  107 us (13%)
  other arithmetic  31.5 us (4%)
  between operations  16.9 us (2%)
    psum x1, waiting for transfers between devices, per_device(): grad_conv, grad_down = lax.psum((grad_conv, grad_down), ('space', 'rep'))  256 us
    ppermute x48, starting transfers between devices, shifted(): lax.ppermute(value, axis, [(source, source + steps) for source in range(i...  148 us
    scatter-add x19, local copies, waits for them, and re-layouts, per_device(): grad_padded = grad_padded.at[:, start_x:start_x + 8, start_y:start_y + 8,...  146 us
    dot_general x27, matrix products, per_device(): jnp.einsum('rd,cd->rc', grad_pre, w_conv[tap_id], preferred_element_type=...  54.6 us
    ppermute x48, waiting for transfers between devices, shifted(): lax.ppermute(value, axis, [(source, source + steps) for source in range(i...  41.2 us
    dot_general x27, matrix products, per_device(): jnp.einsum('rc,rd->cd', window, grad_pre, preferred_element_type=jnp.floa...  26.4 us
  transfers between devices with their start and end apart: 49, of which 22 were waited for; matrix products, arithmetic and copies ran while one was open for 6% of the time, Pallas kernels for 0%

commit v1 on v0

v1 whole, which is shorter than its diff:
```python
import jax
import jax.numpy as jnp
import numpy as np
from jax import lax
from jax.experimental import pallas as pl
from jax.experimental.pallas import tpu as pltpu
from jax.sharding import PartitionSpec as P

BF = jnp.bfloat16
F32 = jnp.float32
MESH = pl.DeviceIdType.MESH
SHIFTS = (-2, -1, 1, 2)
N_SPACE = 64
N_PLANE = 16
N_Z = 8


def onehot_tables():
    tables = {}

    def table(name, rows, cols):
        tables[name] = np.zeros((rows, cols), np.float32)
        return tables[name]

    swap = table("swap", 256, 256)
    for p in range(16):
        for q in range(16):
            swap[p * 16 + q, q * 16 + p] = 1
    send_y, recv_y = table("send_y", 192, 256), table("recv_y", 256, 256)
    send_z, recv_z = table("send_z", 256, 384), table("recv_z", 320, 256)
    send_gz, recv_gz = table("send_gz", 128, 128), table("recv_gz", 128, 128)
    send_gy, recv_gy = table("send_gy", 192, 256), table("recv_gy", 160, 256)
    send_gx = table("send_gx", 128, 256)
    low, high = table("low", 256, 256), table("high", 256, 256)
    insert = table("insert", 512, 128)
    for b in range(4):
        for xq in range(4):
            row = xq * 4 + b
            for z in range(8):
                send_y[b * 48 + xq * 8 + z, z * 16 + row] = 1
                recv_y[z * 16 + row, b * 64 + xq * 8 + z] = 1
                far = (xq + 1) * 8 + z if xq < 3 else 40 + z
                recv_y[128 + z * 16 + row, b * 64 + far] = 1
                if xq == 3:
                    send_y[b * 48 + 40 + z, 128 + z * 16 + row] = 1
                send_gz[b * 32 + z * 4 + xq, z * 16 + row] = 1
                recv_gz[z * 16 + row, b * 32 + z * 4 + xq] = 1
            for y in range(10):
                send_z[b * 64 + xq * 10 + y, y * 16 + row] = 1
                recv_z[y * 16 + row, b * 64 + xq * 10 + y] = 1
                far = (xq + 1) * 10 + y if xq < 3 else 40 + y
                recv_z[160 + y * 16 + row, b * 64 + far] = 1
                if xq == 3:
                    send_z[b * 64 + 40 + y, 160 + y * 16 + row] = 1
                send_gy[b * 48 + y * 4 + xq, y * 16 + row] = 1
                recv_gy[y * 16 + row, b * 64 + y * 4 + xq] = 1
            for k in range(16):
                if xq >= 1:
                    low[k * 16 + row, k * 16 + row - 4] = 1
                if xq <= 2:
                    high[k * 16 + row, k * 16 + row + 4] = 1
        for k in range(16):
            send_gx[b * 16 + k, k * 16 + 12 + b] = 1
            send_gx[64 + b * 16 + k, k * 16 + b] = 1
            insert[k * 16 + b, b * 16 + k] = 1
            insert[256 + k * 16 + 12 + b, 64 + b * 16 + k] = 1
    places, parts, start = {}, [], 0
    for name, value in tables.items():
        rows, cols = value.shape
        places[name] = (start, rows, cols)
        parts.append(np.pad(value, ((0, 0), (0, 384 - cols))))
        start += rows
    return places, np.concatenate(parts)


PLACES, TABLES = onehot_tables()


def mm(left, right):
    return jnp.dot(left, right, preferred_element_type=F32)


def mm_nt(left, right):
    return lax.dot_general(left, right, (((1,), (1,)), ((), ())), preferred_element_type=F32)


def kernel(
    feats_h, wc_h, wd_h, cot_h, tab_h, own_s, slot_s,
    pooled_o, dfeats_o, sums_o,
    feats, wc, wd, cot, tab, bf, bg, wf, wb, gh, hid, gpt, cotp, dwf,
    sx, rx, oy, sy, ry, oz, sz, rz, ogz, sgz, rgz, ogy, sgy, rgy, ogx, sgx, rgx,
    s1, r1, s2, r2, r3, fin,
    lsem, hs, hr, cs, cr, xs, xr, zs, zr, as_, ar, fs, fr,
):
    pos = lax.axis_index("space")
    rep = lax.axis_index("rep")
    core = lax.rem(pos, 2)
    zpos = lax.rem(lax.div(pos, 2), 8)
    xpos = lax.div(pos, 16)
    plane = xpos * 4 + rep
    sibling = pos + 1 - 2 * core

    def in_space(to):
        return {"space": to, "rep": rep}

    def in_plane(k):
        to = lax.rem(plane + k, N_PLANE)
        return {"space": lax.div(to, 4) * 16 + lax.rem(pos, 16), "rep": lax.rem(to, 4)}

    def in_z(k):
        to = lax.rem(zpos + k, N_Z)
        return {"space": xpos * 16 + to * 2 + core, "rep": rep}

    loads = [
        pltpu.make_async_copy(src, dst, lsem.at[i])
        for i, (src, dst) in enumerate(
            ((feats_h, feats), (tab_h, tab), (cot_h, cot), (wc_h, wc), (wd_h, wd))
        )
    ]
    for one in loads:
        one.start()

    barrier = pltpu.get_barrier_semaphore()
    for t in SHIFTS:
        to = lax.rem(pos + t + N_SPACE, N_SPACE)
        pl.semaphore_signal(barrier, inc=1, device_id=in_space(to), device_id_type=MESH)
    pl.semaphore_signal(barrier, inc=1, device_id=in_space(sibling), device_id_type=MESH)

    def greet_plane(k, carry):
        pl.semaphore_signal(barrier, inc=1, device_id=in_plane(k), device_id_type=MESH)
        return carry

    def greet_z(k, carry):
        pl.semaphore_signal(barrier, inc=1, device_id=in_z(k), device_id_type=MESH)
        return carry

    lax.fori_loop(1, N_PLANE, greet_plane, 0)
    lax.fori_loop(1, N_Z, greet_z, 0)

    owners = [[own_s[0, b, d] for d in range(6)] for b in range(4)]
    slots = [[slot_s[0, b, d] for d in range(6)] for b in range(4)]

    def pick(d, t):
        found = jnp.int32(0)
        for b in range(1, 4):
            hit = (owners[b][d] == pos + t) & (owners[b][d] >= 0)
            found = jnp.where(hit, b, found)
        return found

    def place(d, b):
        gap = pos - owners[b][d]
        far = jnp.clip(jnp.where(gap < 0, gap + 2, gap + 1), 0, 3)
        near = jnp.clip(5 + slots[b][d], 5, 8)
        return jnp.where(owners[b][d] < 0, 4, jnp.where(gap == 0, near, far))

    for ref in (rx, ry, rz, rgz, rgy, rgx):
        for side in range(2):
            ref[side, 4] = jnp.zeros(ref.shape[2:], BF)

    def halo_copy(phase, side, i, send, recv):
        to = lax.rem(pos + SHIFTS[i] + N_SPACE, N_SPACE)
        return pltpu.make_async_remote_copy(
            src_ref=send.at[side, i],
            dst_ref=recv.at[side, i],
            send_sem=hs.at[phase, side, i],
            recv_sem=hr.at[phase, side, i],
            device_id=in_space(to),
            device_id_type=MESH,
        )

    sent = []

    def halo_send(phase, axis, own, send, recv):
        copies = []
        for side in range(2):
            for i, t in enumerate(SHIFTS):
                send[side, i] = own(side, pick(2 * axis + side, t))
                one = halo_copy(phase, side, i, send, recv)
                one.start()
                copies.append(one)
        sent.extend(copies)
        return copies

    def halo_recv(axis, copies, recv):
        for one in copies:
            one.wait_recv()
        return [
            [recv[side, place(2 * axis + 1 - side, b)] for b in range(4)] for side in range(2)
        ]

    def onehot(name):
        start, rows, cols = PLACES[name]
        return tab[start : start + rows, 0:cols]

    def permuted(name, value):
        return mm(onehot(name), value).astype(BF)

    loads[0].wait()
    for b in range(4):
        rx[0, 5 + b] = feats[b, 448:512, :]
        rx[1, 5 + b] = feats[b, 0:64, :]
    for side in range(2):
        for i, t in enumerate(SHIFTS):
            rows = slice(448, 512) if side == 0 else slice(0, 64)
            sx[side, i] = feats[pick(side, t), rows, :]
    pl.semaphore_wait(barrier, 4 + 1 + N_PLANE - 1 + N_Z - 1)
    copies = [halo_copy(0, side, i, sx, rx) for side in range(2) for i in range(4)]
    for one in copies:
        one.start()
    sent.extend(copies)

    loads[1].wait()

    def x_layer(s, chunk, halo):
        rows = []
        for xq in range(4):
            x = 2 * xq + s - 1
            for b in range(4):
                if x < 0 or x > 7:
                    rows.append(halo[0 if x < 0 else 1][b][16 * chunk : 16 * chunk + 16])
                else:
                    rows.append(feats[b, 64 * x + 16 * chunk : 64 * x + 16 * chunk + 16, :])
        return jnp.concatenate(rows, axis=0)

    def put_rows(ref, y, z, count, lanes, value):
        ref[pl.ds(y * 10 + z, count), :, lanes] = value

    for chunk in range(4):
        both = jnp.concatenate([x_layer(1, chunk, None), x_layer(2, chunk, None)], axis=1)
        out = permuted("swap", both).reshape(2, 8, 16, 256)
        for j in range(2):
            put_rows(bf, 2 * chunk + j + 1, 1, 8, slice(128, 384), out[j])

    halo = halo_recv(0, copies, rx)
    for chunk in range(4):
        both = jnp.concatenate([x_layer(0, chunk, halo), x_layer(3, chunk, halo)], axis=1)
        out = permuted("swap", both).reshape(2, 8, 16, 256)
        for j in range(2):
            put_rows(bf, 2 * chunk + j + 1, 1, 8, slice(0, 128), out[j, :, :, 0:128])
            put_rows(bf, 2 * chunk + j + 1, 1, 8, slice(384, 512), out[j, :, :, 128:256])

    for side in range(2):
        y = 8 if side == 0 else 1
        layer = bf[y * 10 + 1 : y * 10 + 9].reshape(128, 512)
        flat = jnp.concatenate([layer[:, 0:256], layer[:, 256:512]], axis=0)
        faces = permuted("send_y", flat).reshape(4, 48, 256)
        oy[side] = faces
        ry[side, 5:9] = faces
    copies = halo_send(1, 1, lambda side, b: oy[side, b], sy, ry)

    loads[2].wait()
    loads[3].wait()
    loads[4].wait()
    cot_rows = jnp.concatenate(
        [cot[b, 16 * xq : 16 * xq + 16, :] for xq in range(4) for b in range(4)], axis=0
    )
    cot_perm = permuted("swap", cot_rows)
    cotp[...] = cot_perm

    def down_weight(j, k):
        return jnp.concatenate([wd[2 * j + k], wd[4 + 2 * j + k]], axis=0)

    for j in range(2):
        for k in range(2):
            gh[j, k] = mm_nt(cot_perm, down_weight(j, k)).reshape(4, 64, 256)

    def weights(k9, carry):
        for s in range(4):
            for xl in range(2):
                dx = s - xl
                fwd_at = (pl.ds(s * 128, 128), pl.ds(xl * 128, 128))
                bwd_at = (pl.ds(xl * 128, 128), pl.ds(s * 128, 128))
                if 0 <= dx <= 2:
                    wf[(k9,) + fwd_at] = wc[9 * dx + k9]
                    wb[(k9,) + bwd_at] = wc[9 * (2 - dx) + 8 - k9]
                else:
                    wf[(k9,) + fwd_at] = jnp.zeros((128, 128), BF)
                    wb[(k9,) + bwd_at] = jnp.zeros((128, 128), BF)
        return carry

    lax.fori_loop(0, 9, weights, 0)

    def tall(values, rows):
        pad = jnp.zeros((rows - values[0].shape[0], values[0].shape[1]), BF)
        return jnp.concatenate([v for value in values for v in (value, pad)], axis=0)

    halo = halo_recv(1, copies, ry)
    for side in range(2):
        y = 0 if side == 0 else 9
        out = permuted("recv_y", tall(halo[side], 64))
        put_rows(bf, y, 1, 8, slice(0, 256), out[0:128].reshape(8, 16, 256))
        put_rows(bf, y, 1, 8, slice(256, 512), out[128:256].reshape(8, 16, 256))

    for side in range(2):
        z = 8 if side == 0 else 1
        near = [bf[y * 10 + z, :, 0:256] for y in range(10)]
        far = [bf[y * 10 + z, :, 256:512] for y in range(10)]
        flat = jnp.concatenate(near + far + [jnp.zeros((64, 256), BF)], axis=0)
        faces = permuted("send_z", flat).reshape(4, 64, 256)
        oz[side] = faces
        rz[side, 5:9] = faces
    copies = halo_send(2, 2, lambda side, b: oz[side, b], sz, rz)
    bg[100:112] = jnp.zeros((12, 16, 512), BF)
    dwf[2, 1, 5] = jnp.zeros((128, 128), F32)
    halo = halo_recv(2, copies, rz)
    for side in range(2):
        z = 0 if side == 0 else 9
        out = permuted("recv_z", jnp.concatenate(halo[side], axis=0))
        for y in range(10):
            bf[y * 10 + z, :, 0:256] = out[16 * y : 16 * y + 16]
            bf[y * 10 + z, :, 256:512] = out[160 + 16 * y : 160 + 16 * y + 16]

    def window(ref, y, dz):
        lower = ref[pl.ds(y * 10 + dz, 8)]
        upper = ref[pl.ds(y * 10 + 10 + dz, 8)]
        return jnp.concatenate([lower, upper], axis=0).reshape(256, 512)

    def forward(yq, carry):
        pre = jnp.zeros((256, 256), F32)
        for k9 in range(9):
            pre = pre + mm(window(bf, 2 * yq + k9 // 3, k9 % 3), wf[k9])
        sig = 1.0 / (1.0 + jnp.exp(-pre))
        hidden = (pre * sig).astype(BF).reshape(2, 4, 2, 16, 256)
        grad = []
        for j in range(2):
            for k in range(2):
                hid[j, k, yq] = hidden[j, :, k].reshape(64, 256)
            pair = [gh[j, k, yq].reshape(4, 1, 16, 256) for k in range(2)]
            grad.append(jnp.concatenate(pair, axis=1).reshape(128, 256))
        grad = jnp.concatenate(grad, axis=0) * sig * (1.0 + pre * (1.0 - sig))
        gpt[yq] = grad.T.astype(BF)
        grad = grad.astype(BF).reshape(2, 8, 16, 256)
        for j in range(2):
            bg[pl.ds((2 * yq + j + 1) * 10 + 1, 8), :, 128:384] = grad[j]
        return carry

    lax.fori_loop(0, 4, forward, 0)

    for side in range(2):
        z = 8 if side == 0 else 1
        flat = jnp.concatenate([bg[y * 10 + z, :, 128:384] for y in range(1, 9)], axis=0)
        faces = permuted("send_gz", flat).reshape(4, 32, 256)
        ogz[side] = faces
        rgz[side, 5:9] = faces
    copies = halo_send(3, 2, lambda side, b: ogz[side, b], sgz, rgz)

    def grad_conv(part):
        for dz in range(3):
            first = jnp.zeros((256, 256), F32)
            second = jnp.zeros((256, 256), F32)
            for yq in range(4):
                rows = window(bf, 2 * yq + part, dz)
                first = first + mm(gpt[yq], rows[:, 0:256])
                second = second + mm(gpt[yq], rows[:, 256:512])
            taps = (
                first[0:128, 0:128] + first[128:256, 128:256],
                first[0:128, 128:256] + second[128:256, 0:128],
                second[0:128, 0:128] + second[128:256, 128:256],
            )
            for dx in range(3):
                slot = dx * 3 + dz
                dwf[part, slot // 6, slot % 6] = taps[dx].T

    def core_copy(part):
        return pltpu.make_async_remote_copy(
            src_ref=s1.at[part], dst_ref=r1.at[part], send_sem=cs.at[part], recv_sem=cr.at[part],
            device_id=in_space(sibling), device_id_type=MESH,
        )

    def core_send(part):
        s1[part] = dwf[part, 1 - core].reshape(768, 128).astype(BF)
        core_copy(part).start()

    def plane_copy(part, k):
        return pltpu.make_async_remote_copy(
            src_ref=s2.at[part, lax.rem(plane + k, N_PLANE)], dst_ref=r2.at[part, plane],
            send_sem=xs.at[part, k], recv_sem=xr.at[part, k],
            device_id=in_plane(k), device_id_type=MESH,
        )

    def each(low_k, high_k, act):
        def body(k, carry):
            act(k)
            return carry

        lax.fori_loop(low_k, high_k, body, 0)

    def plane_send(part):
        core_copy(part).wait_recv()
        mine = dwf[part, core].reshape(768, 128) + r1[part].astype(F32)
        s2[part] = mine.astype(BF).reshape(16, 48, 128)
        each(1, N_PLANE, lambda k: plane_copy(part, k).start())
        r2[part, plane] = s2[part, plane]

    def z_copy(part, k):
        return pltpu.make_async_remote_copy(
            src_ref=r3.at[part, zpos], dst_ref=r3.at[part, zpos],
            send_sem=zs.at[part, k], recv_sem=zr.at[part, k],
            device_id=in_z(k), device_id_type=MESH,
        )

    def z_send(part):
        each(1, N_PLANE, lambda k: plane_copy(part, k).wait_recv())
        total = r2[part, 0].astype(F32)
        for i in range(1, N_PLANE):
            total = total + r2[part, i].astype(F32)
        r3[part, zpos] = total.astype(BF)
        each(1, N_Z, lambda k: z_copy(part, k).start())

    def gather_copy(part, k):
        return pltpu.make_async_remote_copy(
            src_ref=fin.at[part], dst_ref=sums_o.at[part, core, plane],
            send_sem=as_.at[part, k], recv_sem=ar.at[part, k],
            device_id=in_plane(k), device_id_type=MESH,
        )

    def hand_copy(part, k):
        at = lax.rem(plane - k + N_PLANE, N_PLANE)
        return pltpu.make_async_remote_copy(
            src_ref=sums_o.at[part, core, at], dst_ref=sums_o.at[part, core, at],
            send_sem=fs.at[part, k], recv_sem=fr.at[part, k],
            device_id=in_space(sibling), device_id_type=MESH,
        )

    def gather_send(part):
        each(1, N_Z, lambda k: z_copy(part, k).wait_recv())
        total = r3[part, 0].astype(F32)
        for i in range(1, N_Z):
            total = total + r3[part, i].astype(F32)
        fin[part] = total.astype(BF)
        each(1, N_PLANE, lambda k: gather_copy(part, k).start())
        sums_o[part, core, plane] = fin[part]
        hand_copy(part, 0).start()

    def hand_over(part):
        def act(k):
            gather_copy(part, k).wait_recv()
            hand_copy(part, k).start()

        each(1, N_PLANE, act)

    def finish(part):
        each(0, N_PLANE, lambda k: hand_copy(part, k).wait_recv())
        core_copy(part).wait_send()
        each(1, N_PLANE, lambda k: plane_copy(part, k).wait_send())
        each(1, N_Z, lambda k: z_copy(part, k).wait_send())
        each(1, N_PLANE, lambda k: gather_copy(part, k).wait_send())
        each(0, N_PLANE, lambda k: hand_copy(part, k).wait_send())

    cot_t = cotp[...].astype(F32).T.astype(BF)
    for j in range(2):
        for k in range(2):
            out = mm(cot_t, hid[j, k].reshape(256, 256))
            for i in range(2):
                tap = 4 * i + 2 * j + k
                dwf[tap // 3, 1, 3 + tap % 3] = out[:, 128 * i : 128 * i + 128].T
    grad_conv(0)
    core_send(0)

    halo = halo_recv(2, copies, rgz)
    for side in range(2):
        z = 0 if side == 0 else 9
        out = permuted("recv_gz", jnp.concatenate(halo[side], axis=0))
        for y in range(8):
            bg[(y + 1) * 10 + z, :, 128:384] = out[16 * y : 16 * y + 16]

    for side in range(2):
        y = 8 if side == 0 else 1
        flat = bg[y * 10 : y * 10 + 10, :, 128:384].reshape(160, 256)
        flat = jnp.concatenate([flat, jnp.zeros((96, 256), BF)], axis=0)
        faces = permuted("send_gy", flat).reshape(4, 48, 256)
        ogy[side] = faces
        rgy[side, 5:9] = faces
    copies = halo_send(4, 1, lambda side, b: ogy[side, b], sgy, rgy)
    plane_send(0)
    grad_conv(1)
    core_send(1)
    halo = halo_recv(1, copies, rgy)
    for side in range(2):
        y = 0 if side == 0 else 9
        out = permuted("recv_gy", tall(halo[side], 64))
        put_rows(bg, y, 0, 10, slice(128, 384), out.reshape(10, 16, 256))

    for group in range(7):
        tiles = bg[16 * group : 16 * group + 16, :, 128:384].reshape(256, 256)
        out = permuted("send_gx", tiles)
        for b in range(4):
            rows = slice(16 * group, 16 * group + 16)
            for side in range(2):
                lanes = slice(128, 256) if side == 0 else slice(0, 128)
                face = out[64 * side + 16 * b : 64 * side + 16 * b + 16, lanes]
                ogx[side, b, rows] = face
                rgx[side, 5 + b, rows] = face
    copies = halo_send(5, 0, lambda side, b: ogx[side, b], sgx, rgx)
    plane_send(1)
    for group in range(7):
        at = slice(16 * group, 16 * group + 16)
        tiles = bg[at, :, 128:384].reshape(256, 256)
        bg[at, :, 0:128] = permuted("low", tiles[:, 128:256]).reshape(16, 16, 128)
        bg[at, :, 384:512] = permuted("high", tiles[:, 0:128]).reshape(16, 16, 128)
    grad_conv(2)
    core_send(2)

    total = jnp.zeros((256, 128), F32)
    for j in range(2):
        for k in range(2):
            total = total + mm(hid[j, k].reshape(256, 256), down_weight(j, k))
    out = permuted("swap", total.astype(BF))
    for b in range(4):
        for xq in range(4):
            at = 16 * (4 * xq + b)
            pooled_o[b, 16 * xq : 16 * xq + 16, :] = out[at : at + 16]

    halo = halo_recv(0, copies, rgx)
    for group in range(7):
        at = slice(16 * group, 16 * group + 16)
        rows = jnp.concatenate([halo[side][b][at] for side in range(2) for b in range(4)], axis=0)
        out = permuted("insert", rows)
        bg[at, :, 0:128] = bg[at, :, 0:128] + out[0:256].reshape(16, 16, 128)
        bg[at, :, 384:512] = bg[at, :, 384:512] + out[256:512].reshape(16, 16, 128)

    plane_send(2)
    z_send(0)

    def backward(yq, carry):
        grad = jnp.zeros((256, 256), F32)
        for k9 in range(9):
            grad = grad + mm_nt(window(bg, 2 * yq + k9 // 3, k9 % 3), wb[k9])
        out = permuted("swap", grad.astype(BF))
        for xq in range(4):
            for b in range(4):
                tile = out[16 * (4 * xq + b) : 16 * (4 * xq + b) + 16]
                for xl in range(2):
                    at = pl.ds(pl.multiple_of(64 * (2 * xq + xl) + 16 * yq, 16), 16)
                    dfeats_o[b, at, :] = tile[:, 128 * xl : 128 * xl + 128]
        return carry

    lax.fori_loop(0, 2, backward, 0)
    gather_send(0)
    z_send(1)
    lax.fori_loop(2, 4, backward, 0)
    gather_send(1)
    z_send(2)
    hand_over(0)
    gather_send(2)
    hand_over(1)
    hand_over(2)
    for one in sent:
        one.wait_send()
    for part in range(3):
        finish(part)


def per_device(feats, w_conv, w_down, cotangent, nbr_owner, nbr_slot):
    vmem = pl.BlockSpec(memory_space=pltpu.VMEM)
    smem = pl.BlockSpec(memory_space=pltpu.SMEM)
    anywhere = pl.BlockSpec(memory_space=pl.ANY)

    def buf(*shape, dtype=BF):
        return pltpu.VMEM(shape, dtype)

    def halo(rows, lanes, own=True):
        bufs = [buf(2, 4, rows, lanes), buf(2, 9, rows, lanes)]
        return ([buf(2, 4, rows, lanes)] if own else []) + bufs

    dma = pltpu.SemaphoreType.DMA
    pooled, d_feats, sums = pl.pallas_call(
        kernel,
        out_shape=(
            jax.ShapeDtypeStruct((4, 64, 128), BF),
            jax.ShapeDtypeStruct((4, 512, 128), BF),
            jax.ShapeDtypeStruct((3, 2, 16, 48, 128), BF),
        ),
        in_specs=[anywhere] * 5 + [smem] * 2,
        out_specs=(vmem, vmem, vmem),
        scratch_shapes=[
            buf(4, 512, 128), buf(27, 128, 128), buf(8, 128, 128), buf(4, 64, 128),
            buf(*TABLES.shape),
            buf(100, 16, 512), buf(112, 16, 512),
            buf(9, 512, 256), buf(9, 256, 512),
            buf(2, 2, 4, 64, 256, dtype=F32), buf(2, 2, 4, 64, 256),
            buf(4, 256, 256), buf(256, 128),
            buf(3, 2, 6, 128, 128, dtype=F32),
            *halo(64, 128, own=False), *halo(48, 256), *halo(64, 256),
            *halo(32, 256), *halo(48, 256), *halo(112, 128),
            buf(3, 768, 128), buf(3, 768, 128),
            buf(3, 16, 48, 128), buf(3, 16, 48, 128), buf(3, 8, 48, 128), buf(3, 48, 128),
            dma((5,)),
            dma((6, 2, 4)), dma((6, 2, 4)),
            dma((3,)), dma((3,)),
            dma((3, 16)), dma((3, 16)),
            dma((3, 8)), dma((3, 8)),
            dma((3, 16)), dma((3, 16)),
            dma((3, 16)), dma((3, 16)),
        ],
        compiler_params=pltpu.CompilerParams(
            collective_id=0, has_side_effects=True, vmem_limit_bytes=48 * 1024 * 1024
        ),
    )(
        feats[0], w_conv, w_down, cotangent[0], jnp.asarray(TABLES, BF), nbr_owner, nbr_slot
    )
    norm_factor = 1.0 / float(lax.axis_size("rep") * lax.axis_size("space") * 4 * 512) ** 0.5
    sums = sums.reshape(3, 12, 128, 128).astype(F32) * norm_factor
    grad_conv = sums[:, 0:9].reshape(3, 3, 3, 128, 128).transpose(1, 0, 2, 3, 4)
    grad_down = sums[:, 9:12].reshape(9, 128, 128)[0:8]
    return (pooled[None], d_feats[None], grad_conv.reshape(27, 128, 128), grad_down)


def solution(mesh):
    placed = (
        P("rep", "space", None, None),
        P(),
        P(),
        P("rep", "space", None, None),
        P("rep", "space", None),
        P("rep", "space", None),
    )
    return jax.shard_map(
        per_device,
        mesh=mesh,
        in_specs=placed,
        out_specs=(P("rep", "space", None, None), P("rep", "space", None, None), P(), P()),
        check_vma=False,
    )
```

time: 815 us -> 88.1 us (0.11); the launches traced: 799 us -> 87.8 us
  waiting for transfers between devices: 297 us -> 0 us
  local copies, waits for them, and re-layouts: 199 us -> 10.9 us
  starting transfers between devices: 148 us -> 0 us
  matrix products: 107 us -> 0 us
  Pallas kernels: 0 us -> 76 us
  other arithmetic: 31.5 us -> 0.23 us
  between operations: 16.9 us -> 0.68 us
    psum x1 -> x0, waiting for transfers between devices: 256 us -> none  [per_device(): grad_conv, grad_down = lax.psum((grad_conv, grad_down), ('space', 'rep'))]
    scatter-add x21 -> x0, local copies, waits for them, and re-layouts: 168 us -> none  [the longest x19 146 us: per_device(): grad_padded = grad_padded.at[:, start_x:start_x + 8, start_y:start_y + 8,...]
    ppermute x48 -> x0, starting transfers between devices: 148 us -> none  [shifted(): lax.ppermute(value, axis, [(source, source + steps) for source in range(i...]
    dot_general x114 -> x0, matrix products: 107 us -> none  [the longest x27 54.6 us: per_device(): jnp.einsum('rd,cd->rc', grad_pre, w_conv[tap_id], preferred_element_type=...]
    pallas_call x0 -> x1, Pallas kernels: none -> 76 us  [per_device(): pl.pallas_call(kernel, out_shape=(jax.ShapeDtypeStruct((4, 64, 128), BF),...]
    ppermute x48 -> x0, waiting for transfers between devices: 41.2 us -> none  [shifted(): lax.ppermute(value, axis, [(source, source + steps) for source in range(i...]
    another operation x60 -> x0, other arithmetic: 15.4 us -> none
    slice x14 -> x3, local copies, waits for them, and re-layouts: 11 us -> 1.05 us  [the longest x2 0.87 us: per_device(): grad_down = sums[:, 9:12].reshape(9, 128, 128)[0:8]]
  transfers between devices with their start and end apart: 49 -> 0, of which waited for: 22 -> 0; matrix products, arithmetic and copies ran while one was open for 6% -> 0% of each run, Pallas kernels for 0% -> 0%
where the time goes in v1:
time: 88.1 us; the launch traced here: 87.8 us
  Pallas kernels  76 us (86%)
  local copies, waits for them, and re-layouts  10.9 us (12%)
    pallas_call x1, Pallas kernels, per_device(): pl.pallas_call(kernel, out_shape=(jax.ShapeDtypeStruct((4, 64, 128), BF),...  76 us
    unnamed x16, local copies, waits for them, and re-layouts  8.43 us

profile of v1, /device:TPU:1, one launch (start us, length us, event | category | flops | bytes accessed | tf_op | source)
XLA Modules:
  0.0 87.8 jit_solution(11836094497407411555)
XLA Ops:
  0.6 0.0 copy-start
  0.6 1.6 %copy-done = bf16[3040,384]{1,0:T(8,128)(2,1)S(1)} copy-done((bf16[3040,384]{1,0:T(8,128)(2,1)S(1)}, bf16[3040,384]{1,0:T(8,128)(2,1)}, u32[]{:S(2)}) %copy-start) | copy-done | bytes 2334744
  2.3 0.0 copy-start.1
  2.3 1.2 %copy-done.1 = bf16[27,128,128]{2,1,0:T(8,128)(2,1)S(1)} copy-done((bf16[27,128,128]{2,1,0:T(8,128)(2,1)S(1)}, bf16[27,128,128]{2,1,0:T(8,128)(2,1)}, u32[]{:S(2)}) %copy-start.1) | copy-done | bytes 884760
  3.5 0.0 copy-start.2
  3.5 1.0 %copy-done.2 = bf16[1,4,512,128]{3,2,1,0:T(8,128)(2,1)S(1)} copy-done((bf16[1,4,512,128]{3,2,1,0:T(8,128)(2,1)S(1)}, bf16[1,4,512,128]{3,2,1,0:T(8,128)(2,1)}, u32[]{:S(2)}) %copy-start.2) | copy-done | bytes 524312
  4.5 0.0 copy-start.3
  4.5 0.9 %copy-done.3 = bf16[8,128,128]{2,1,0:T(8,128)(2,1)S(1)} copy-done((bf16[8,128,128]{2,1,0:T(8,128)(2,1)S(1)}, bf16[8,128,128]{2,1,0:T(8,128)(2,1)}, u32[]{:S(2)}) %copy-start.3) | copy-done | bytes 262168
  5.5 0.0 copy-start.4
  5.5 0.8 copy-done.4
  6.3 0.0 copy-start.5
  6.3 0.7 copy-done.5
  7.0 0.0 copy-start.6
  7.0 0.7 copy-done.6
  7.7 76.0 %shard_map.102 = (bf16[4,64,128]{2,1,0:T(8,128)(2,1)S(1)}, bf16[4,512,128]{2,1,0:T(8,128)(2,1)S(1)}, bf16[3,2,16,48,128]{4,3,2,1,0:T(8,128)(2,1)S(1)}) custom-call(bf16[4,512,128]{2,1,0:T(8,128)(2,1)S(1)} %bitcast.10, bf16[27,128,128]{2,1,0:T(8,128)(2,1)S(1)} %copy-done.1, bf16[8,128,128]{2,1,0:T(8,128)(2,1)S(1)} %copy-done.3, ...), custom_call_target="tpu_custom_call" | custom-call | tf_op jit(solution)/shard_map/pallas_call | solution.py:567
  83.6 0.2 convert_multiply_fusion
  83.9 0.2 slice.12
  84.1 1.4 %copy.11 = f32[3,3,3,128,128]{4,3,2,0,1:T(8,128)} copy(f32[3,3,3,128,128]{4,3,2,1,0:T(8,128)S(1)} %bitcast.16) | data formatting | bytes 3538944 | tf_op jit(solution)/shard_map/reshape | solution.py:604
  85.5 0.8 slice.14
  86.3 0.6 copy.14
  87.0 0.8 copy.15
  (1 shorter events, 0.0 us)
Async XLA Ops:
  0.6 1.7 %copy-start = (bf16[3040,384]{1,0:T(8,128)(2,1)S(1)}, bf16[3040,384]{1,0:T(8,128)(2,1)}, u32[]{:S(2)}) copy-start(bf16[3040,384]{1,0:T(8,128)(2,1)} %constant.4.clone.tab_h) | copy-start | bytes 7004164
  2.3 1.2 %copy-start.1 = (bf16[27,128,128]{2,1,0:T(8,128)(2,1)S(1)}, bf16[27,128,128]{2,1,0:T(8,128)(2,1)}, u32[]{:S(2)}) copy-start(bf16[27,128,128]{2,1,0:T(8,128)(2,1)} %wc_h.1) | copy-start | bytes 2654212
  3.5 1.0 %copy-start.2 = (bf16[1,4,512,128]{3,2,1,0:T(8,128)(2,1)S(1)}, bf16[1,4,512,128]{3,2,1,0:T(8,128)(2,1)}, u32[]{:S(2)}) copy-start(bf16[1,4,512,128]{3,2,1,0:T(8,128)(2,1)} %param.7) | copy-start | bytes 1572868
  4.5 0.9 %copy-start.3 = (bf16[8,128,128]{2,1,0:T(8,128)(2,1)S(1)}, bf16[8,128,128]{2,1,0:T(8,128)(2,1)}, u32[]{:S(2)}) copy-start(bf16[8,128,128]{2,1,0:T(8,128)(2,1)} %wd_h.1) | copy-start | bytes 786436
  5.5 0.8 copy-start.4
  6.3 0.7 copy-start.5
  7.0 0.7 copy-start.6

commit v2 on v1

--- a/solution.py
+++ b/solution.py
@@ -1,3 +1,5 @@
+import functools
+
 import jax
 import jax.numpy as jnp
 import numpy as np
@@ -85,9 +87,9 @@
 
 
 def kernel(
-    feats_h, wc_h, wd_h, cot_h, tab_h, own_s, slot_s,
+    feats_h, wc_h, wd_h, cot_h, tab_h, own_h, slot_h,
     pooled_o, dfeats_o, sums_o,
-    feats, wc, wd, cot, tab, bf, bg, wf, wb, gh, hid, gpt, cotp, dwf,
+    feats, wc, wd, cot, tab, own_s, slot_s, bf, bg, wf, wb, gh, hid, gpt, cotp, dwf,
     sx, rx, oy, sy, ry, oz, sz, rz, ogz, sgz, rgz, ogy, sgy, rgy, ogx, sgx, rgx,
     s1, r1, s2, r2, r3, fin,
     lsem, hs, hr, cs, cr, xs, xr, zs, zr, as_, ar, fs, fr,
@@ -114,7 +116,10 @@
     loads = [
         pltpu.make_async_copy(src, dst, lsem.at[i])
         for i, (src, dst) in enumerate(
-            ((feats_h, feats), (tab_h, tab), (cot_h, cot), (wc_h, wc), (wd_h, wd))
+            (
+                (own_h, own_s), (slot_h, slot_s), (feats_h, feats), (tab_h, tab),
+                (cot_h, cot), (wc_h, wc), (wd_h, wd),
+            )
         )
     ]
     for one in loads:
@@ -136,6 +141,9 @@
 
     lax.fori_loop(1, N_PLANE, greet_plane, 0)
     lax.fori_loop(1, N_Z, greet_z, 0)
+
+    loads[0].wait()
+    loads[1].wait()
 
     owners = [[own_s[0, b, d] for d in range(6)] for b in range(4)]
     slots = [[slot_s[0, b, d] for d in range(6)] for b in range(4)]
@@ -154,16 +162,15 @@
         return jnp.where(owners[b][d] < 0, 4, jnp.where(gap == 0, near, far))
 
     for ref in (rx, ry, rz, rgz, rgy, rgx):
-        for side in range(2):
-            ref[side, 4] = jnp.zeros(ref.shape[2:], BF)
-
-    def halo_copy(phase, side, i, send, recv):
+        ref[4] = jnp.zeros(ref.shape[1:], BF)
+
+    def halo_copy(phase, i, send, recv):
         to = lax.rem(pos + SHIFTS[i] + N_SPACE, N_SPACE)
         return pltpu.make_async_remote_copy(
-            src_ref=send.at[side, i],
-            dst_ref=recv.at[side, i],
-            send_sem=hs.at[phase, side, i],
-            recv_sem=hr.at[phase, side, i],
+            src_ref=send.at[i],
+            dst_ref=recv.at[i],
+            send_sem=hs.at[phase, i],
+            recv_sem=hr.at[phase, i],
             device_id=in_space(to),
             device_id_type=MESH,
         )
@@ -172,12 +179,12 @@
 
     def halo_send(phase, axis, own, send, recv):
         copies = []
-        for side in range(2):
-            for i, t in enumerate(SHIFTS):
-                send[side, i] = own(side, pick(2 * axis + side, t))
-                one = halo_copy(phase, side, i, send, recv)
-                one.start()
-                copies.append(one)
+        for i, t in enumerate(SHIFTS):
+            for side in range(2):
+                send[i, side] = own(side, pick(2 * axis + side, t))
+            one = halo_copy(phase, i, send, recv)
+            one.start()
+            copies.append(one)
         sent.extend(copies)
         return copies
 
@@ -185,7 +192,7 @@
         for one in copies:
             one.wait_recv()
         return [
-            [recv[side, place(2 * axis + 1 - side, b)] for b in range(4)] for side in range(2)
+            [recv[place(2 * axis + 1 - side, b), side] for b in range(4)] for side in range(2)
         ]
 
     def onehot(name):
@@ -195,21 +202,21 @@
     def permuted(name, value):
         return mm(onehot(name), value).astype(BF)
 
-    loads[0].wait()
+    loads[2].wait()
     for b in range(4):
-        rx[0, 5 + b] = feats[b, 448:512, :]
-        rx[1, 5 + b] = feats[b, 0:64, :]
+        rx[5 + b, 0] = feats[b, 448:512, :]
+        rx[5 + b, 1] = feats[b, 0:64, :]
     for side in range(2):
         for i, t in enumerate(SHIFTS):
             rows = slice(448, 512) if side == 0 else slice(0, 64)
-            sx[side, i] = feats[pick(side, t), rows, :]
+            sx[i, side] = feats[pick(side, t), rows, :]
     pl.semaphore_wait(barrier, 4 + 1 + N_PLANE - 1 + N_Z - 1)
-    copies = [halo_copy(0, side, i, sx, rx) for side in range(2) for i in range(4)]
+    copies = [halo_copy(0, i, sx, rx) for i in range(4)]
     for one in copies:
         one.start()
     sent.extend(copies)
 
-    loads[1].wait()
+    loads[3].wait()
 
     def x_layer(s, chunk, halo):
         rows = []
@@ -245,12 +252,11 @@
         flat = jnp.concatenate([layer[:, 0:256], layer[:, 256:512]], axis=0)
         faces = permuted("send_y", flat).reshape(4, 48, 256)
         oy[side] = faces
-        ry[side, 5:9] = faces
+        ry[5:9, side] = faces
     copies = halo_send(1, 1, lambda side, b: oy[side, b], sy, ry)
 
-    loads[2].wait()
-    loads[3].wait()
-    loads[4].wait()
+    for one in loads[4:]:
+        one.wait()
     cot_rows = jnp.concatenate(
         [cot[b, 16 * xq : 16 * xq + 16, :] for xq in range(4) for b in range(4)], axis=0
     )
@@ -262,7 +268,9 @@
 
     for j in range(2):
         for k in range(2):
-            gh[j, k] = mm_nt(cot_perm, down_weight(j, k)).reshape(4, 64, 256)
+            out = mm_nt(cot_perm, down_weight(j, k)).reshape(4, 4, 16, 256)
+            for zq in range(4):
+                gh[j, 2 * zq + k] = out[:, zq]
 
     def weights(k9, carry):
         for s in range(4):
@@ -298,10 +306,34 @@
         flat = jnp.concatenate(near + far + [jnp.zeros((64, 256), BF)], axis=0)
         faces = permuted("send_z", flat).reshape(4, 64, 256)
         oz[side] = faces
-        rz[side, 5:9] = faces
+        rz[5:9, side] = faces
     copies = halo_send(2, 2, lambda side, b: oz[side, b], sz, rz)
     bg[100:112] = jnp.zeros((12, 16, 512), BF)
     dwf[2, 1, 5] = jnp.zeros((128, 128), F32)
+    def window(ref, y, z, count):
+        lower = ref[pl.ds(y * 10 + z, count)]
+        upper = ref[pl.ds(y * 10 + 10 + z, count)]
+        return jnp.concatenate([lower, upper], axis=0).reshape(32 * count, 512)
+
+    def activate(pre, grad):
+        sig = 1.0 / (1.0 + jnp.exp(-pre))
+        hidden = (pre * sig).astype(BF).reshape(-1, 16, 256)
+        grad = (grad * sig * (1.0 + pre * (1.0 - sig))).astype(BF)
+        return hidden, grad.reshape(-1, 16, 256)
+
+    def inner(yq, carry):
+        pre = jnp.zeros((192, 256), F32)
+        for k9 in range(9):
+            pre = pre + mm(window(bf, 2 * yq + k9 // 3, 1 + k9 % 3, 6), wf[k9])
+        grad = jnp.concatenate([gh[j, 1:7, yq] for j in range(2)], axis=0).reshape(192, 256)
+        hidden, grad = activate(pre, grad)
+        for j in range(2):
+            hid[j, 1:7, yq] = hidden[6 * j : 6 * j + 6]
+            bg[pl.ds((2 * yq + j + 1) * 10 + 2, 6), :, 128:384] = grad[6 * j : 6 * j + 6]
+        return carry
+
+    lax.fori_loop(0, 4, inner, 0)
+
     halo = halo_recv(2, copies, rz)
     for side in range(2):
         z = 0 if side == 0 else 9
@@ -310,38 +342,23 @@
             bf[y * 10 + z, :, 0:256] = out[16 * y : 16 * y + 16]
             bf[y * 10 + z, :, 256:512] = out[160 + 16 * y : 160 + 16 * y + 16]
 
-    def window(ref, y, dz):
-        lower = ref[pl.ds(y * 10 + dz, 8)]
-        upper = ref[pl.ds(y * 10 + 10 + dz, 8)]
-        return jnp.concatenate([lower, upper], axis=0).reshape(256, 512)
-
-    def forward(yq, carry):
-        pre = jnp.zeros((256, 256), F32)
-        for k9 in range(9):
-            pre = pre + mm(window(bf, 2 * yq + k9 // 3, k9 % 3), wf[k9])
-        sig = 1.0 / (1.0 + jnp.exp(-pre))
-        hidden = (pre * sig).astype(BF).reshape(2, 4, 2, 16, 256)
-        grad = []
-        for j in range(2):
-            for k in range(2):
-                hid[j, k, yq] = hidden[j, :, k].reshape(64, 256)
-            pair = [gh[j, k, yq].reshape(4, 1, 16, 256) for k in range(2)]
-            grad.append(jnp.concatenate(pair, axis=1).reshape(128, 256))
-        grad = jnp.concatenate(grad, axis=0) * sig * (1.0 + pre * (1.0 - sig))
-        gpt[yq] = grad.T.astype(BF)
-        grad = grad.astype(BF).reshape(2, 8, 16, 256)
-        for j in range(2):
-            bg[pl.ds((2 * yq + j + 1) * 10 + 1, 8), :, 128:384] = grad[j]
-        return carry
-
-    lax.fori_loop(0, 4, forward, 0)
+    outer = [(y, z) for y in range(8) for z in (0, 7)]
+    pre = jnp.zeros((256, 256), F32)
+    for k9 in range(9):
+        tiles = [bf[(y + k9 // 3) * 10 + z + k9 % 3] for y, z in outer]
+        pre = pre + mm(jnp.concatenate(tiles, axis=0), wf[k9])
+    grad = jnp.concatenate([gh[y % 2, z, y // 2] for y, z in outer], axis=0)
+    hidden, grad = activate(pre, grad)
+    for at, (y, z) in enumerate(outer):
+        hid[y % 2, z, y // 2] = hidden[at]
+        bg[(y + 1) * 10 + z + 1, :, 128:384] = grad[at]
 
     for side in range(2):
         z = 8 if side == 0 else 1
         flat = jnp.concatenate([bg[y * 10 + z, :, 128:384] for y in range(1, 9)], axis=0)
         faces = permuted("send_gz", flat).reshape(4, 32, 256)
         ogz[side] = faces
-        rgz[side, 5:9] = faces
+        rgz[5:9, side] = faces
     copies = halo_send(3, 2, lambda side, b: ogz[side, b], sgz, rgz)
 
     def grad_conv(part):
@@ -349,7 +366,7 @@
             first = jnp.zeros((256, 256), F32)
             second = jnp.zeros((256, 256), F32)
             for yq in range(4):
-                rows = window(bf, 2 * yq + part, dz)
+                rows = window(bf, 2 * yq + part, dz, 8)
                 first = first + mm(gpt[yq], rows[:, 0:256])
                 second = second + mm(gpt[yq], rows[:, 256:512])
             taps = (
@@ -374,7 +391,7 @@
     def plane_copy(part, k):
         return pltpu.make_async_remote_copy(
             src_ref=s2.at[part, lax.rem(plane + k, N_PLANE)], dst_ref=r2.at[part, plane],
-            send_sem=xs.at[part, k], recv_sem=xr.at[part, k],
+            send_sem=xs.at[part], recv_sem=xr.at[part],
             device_id=in_plane(k), device_id_type=MESH,
         )
 
@@ -395,12 +412,12 @@
     def z_copy(part, k):
         return pltpu.make_async_remote_copy(
             src_ref=r3.at[part, zpos], dst_ref=r3.at[part, zpos],
-            send_sem=zs.at[part, k], recv_sem=zr.at[part, k],
+            send_sem=zs.at[part], recv_sem=zr.at[part],
             device_id=in_z(k), device_id_type=MESH,
         )
 
     def z_send(part):
-        each(1, N_PLANE, lambda k: plane_copy(part, k).wait_recv())
+        all_bytes(r2.at[part, 0 : N_PLANE - 1], xr.at[part])
         total = r2[part, 0].astype(F32)
         for i in range(1, N_PLANE):
             total = total + r2[part, i].astype(F32)
@@ -410,52 +427,59 @@
     def gather_copy(part, k):
         return pltpu.make_async_remote_copy(
             src_ref=fin.at[part], dst_ref=sums_o.at[part, core, plane],
-            send_sem=as_.at[part, k], recv_sem=ar.at[part, k],
+            send_sem=as_.at[part], recv_sem=ar.at[part],
             device_id=in_plane(k), device_id_type=MESH,
         )
 
-    def hand_copy(part, k):
-        at = lax.rem(plane - k + N_PLANE, N_PLANE)
+    def hand_copy(part):
+        half = sums_o.at[part, core]
         return pltpu.make_async_remote_copy(
-            src_ref=sums_o.at[part, core, at], dst_ref=sums_o.at[part, core, at],
-            send_sem=fs.at[part, k], recv_sem=fr.at[part, k],
+            src_ref=half, dst_ref=half, send_sem=fs.at[part], recv_sem=fr.at[part],
             device_id=in_space(sibling), device_id_type=MESH,
         )
 
+    def all_bytes(ref, sem):
+        pltpu.make_async_copy(ref, ref, sem).wait()
+
     def gather_send(part):
-        each(1, N_Z, lambda k: z_copy(part, k).wait_recv())
+        all_bytes(r3.at[part, 0 : N_Z - 1], zr.at[part])
         total = r3[part, 0].astype(F32)
         for i in range(1, N_Z):
             total = total + r3[part, i].astype(F32)
         fin[part] = total.astype(BF)
         each(1, N_PLANE, lambda k: gather_copy(part, k).start())
         sums_o[part, core, plane] = fin[part]
-        hand_copy(part, 0).start()
 
     def hand_over(part):
-        def act(k):
-            gather_copy(part, k).wait_recv()
-            hand_copy(part, k).start()
-
-        each(1, N_PLANE, act)
+        all_bytes(sums_o.at[part, core, 0 : N_PLANE - 1], ar.at[part])
+        hand_copy(part).start()
 
     def finish(part):
-        each(0, N_PLANE, lambda k: hand_copy(part, k).wait_recv())
+        hand_copy(part).wait_recv()
         core_copy(part).wait_send()
-        each(1, N_PLANE, lambda k: plane_copy(part, k).wait_send())
-        each(1, N_Z, lambda k: z_copy(part, k).wait_send())
-        each(1, N_PLANE, lambda k: gather_copy(part, k).wait_send())
-        each(0, N_PLANE, lambda k: hand_copy(part, k).wait_send())
-
+        all_bytes(s2.at[part, 0 : N_PLANE - 1], xs.at[part])
+        all_bytes(r3.at[part, 0 : N_Z - 1], zs.at[part])
+        all_bytes(sums_o.at[part, core, 0 : N_PLANE - 1], as_.at[part])
+        hand_copy(part).wait_send()
+
+    def down_rows(j, k):
+        tiles = [hid[j, 2 * zq + k, yq] for yq in range(4) for zq in range(4)]
+        return jnp.concatenate(tiles, axis=0)
+
+    for yq in range(4):
+        gpt[yq] = window(bg, 2 * yq + 1, 1, 8)[:, 128:384].astype(F32).T.astype(BF)
     cot_t = cotp[...].astype(F32).T.astype(BF)
     for j in range(2):
         for k in range(2):
-            out = mm(cot_t, hid[j, k].reshape(256, 256))
+            out = mm(cot_t, down_rows(j, k))
             for i in range(2):
                 tap = 4 * i + 2 * j + k
                 dwf[tap // 3, 1, 3 + tap % 3] = out[:, 128 * i : 128 * i + 128].T
     grad_conv(0)
     core_send(0)
+    grad_conv(1)
+    core_send(1)
+    plane_send(0)
 
     halo = halo_recv(2, copies, rgz)
     for side in range(2):
@@ -470,11 +494,12 @@
         flat = jnp.concatenate([flat, jnp.zeros((96, 256), BF)], axis=0)
         faces = permuted("send_gy", flat).reshape(4, 48, 256)
         ogy[side] = faces
-        rgy[side, 5:9] = faces
+        rgy[5:9, side] = faces
     copies = halo_send(4, 1, lambda side, b: ogy[side, b], sgy, rgy)
-    plane_send(0)
-    grad_conv(1)
-    core_send(1)
+    grad_conv(2)
+    core_send(2)
+    plane_send(1)
+    plane_send(2)
     halo = halo_recv(1, copies, rgy)
     for side in range(2):
         y = 0 if side == 0 else 9
@@ -490,21 +515,19 @@
                 lanes = slice(128, 256) if side == 0 else slice(0, 128)
                 face = out[64 * side + 16 * b : 64 * side + 16 * b + 16, lanes]
                 ogx[side, b, rows] = face
-                rgx[side, 5 + b, rows] = face
+                rgx[5 + b, side, rows] = face
     copies = halo_send(5, 0, lambda side, b: ogx[side, b], sgx, rgx)
-    plane_send(1)
     for group in range(7):
         at = slice(16 * group, 16 * group + 16)
         tiles = bg[at, :, 128:384].reshape(256, 256)
         bg[at, :, 0:128] = permuted("low", tiles[:, 128:256]).reshape(16, 16, 128)
         bg[at, :, 384:512] = permuted("high", tiles[:, 0:128]).reshape(16, 16, 128)
-    grad_conv(2)
-    core_send(2)
+    z_send(0)
 
     total = jnp.zeros((256, 128), F32)
     for j in range(2):
         for k in range(2):
-            total = total + mm(hid[j, k].reshape(256, 256), down_weight(j, k))
+            total = total + mm(down_rows(j, k), down_weight(j, k))
     out = permuted("swap", total.astype(BF))
     for b in range(4):
         for xq in range(4):
@@ -519,13 +542,13 @@
         bg[at, :, 0:128] = bg[at, :, 0:128] + out[0:256].reshape(16, 16, 128)
         bg[at, :, 384:512] = bg[at, :, 384:512] + out[256:512].reshape(16, 16, 128)
 
-    plane_send(2)
-    z_send(0)
+    z_send(1)
+    z_send(2)
 
     def backward(yq, carry):
         grad = jnp.zeros((256, 256), F32)
         for k9 in range(9):
-            grad = grad + mm_nt(window(bg, 2 * yq + k9 // 3, k9 % 3), wb[k9])
+            grad = grad + mm_nt(window(bg, 2 * yq + k9 // 3, k9 % 3, 8), wb[k9])
         out = permuted("swap", grad.astype(BF))
         for xq in range(4):
             for b in range(4):
@@ -537,12 +560,10 @@
 
     lax.fori_loop(0, 2, backward, 0)
     gather_send(0)
-    z_send(1)
+    gather_send(1)
+    gather_send(2)
     lax.fori_loop(2, 4, backward, 0)
-    gather_send(1)
-    z_send(2)
     hand_over(0)
-    gather_send(2)
     hand_over(1)
     hand_over(2)
     for one in sent:
@@ -551,59 +572,89 @@
         finish(part)
 
 
+def epilogue(norm, sums, pooled, dfeats, pooled_o, dfeats_o, conv_o, down_o, conv, down, sem):
+    copies = [
+        pltpu.make_async_copy(dfeats, dfeats_o, sem.at[0]),
+        pltpu.make_async_copy(pooled, pooled_o, sem.at[1]),
+    ]
+    copies[0].start()
+    copies[1].start()
+    for part in range(3):
+        conv[part] = (sums[part, 0:9].astype(F32) * norm).reshape(3, 3, 128, 128)
+        one = pltpu.make_async_copy(conv.at[part], conv_o.at[:, part], sem.at[2 + part])
+        one.start()
+        copies.append(one)
+    for tap in range(8):
+        down[tap] = sums[tap // 3, 9 + tap % 3].astype(F32) * norm
+    one = pltpu.make_async_copy(down, down_o, sem.at[5])
+    one.start()
+    copies.append(one)
+    for one in copies:
+        one.wait()
+
+
 def per_device(feats, w_conv, w_down, cotangent, nbr_owner, nbr_slot):
-    vmem = pl.BlockSpec(memory_space=pltpu.VMEM)
-    smem = pl.BlockSpec(memory_space=pltpu.SMEM)
-    anywhere = pl.BlockSpec(memory_space=pl.ANY)
-
     def buf(*shape, dtype=BF):
         return pltpu.VMEM(shape, dtype)
 
     def halo(rows, lanes, own=True):
-        bufs = [buf(2, 4, rows, lanes), buf(2, 9, rows, lanes)]
+        bufs = [buf(4, 2, rows, lanes), buf(9, 2, rows, lanes)]
         return ([buf(2, 4, rows, lanes)] if own else []) + bufs
 
+    def in_hbm(value):
+        return pltpu.with_memory_space_constraint(value, pltpu.HBM)
+
+    vmem = pl.BlockSpec(memory_space=pltpu.VMEM)
+    hbm = pl.BlockSpec(memory_space=pltpu.HBM)
     dma = pltpu.SemaphoreType.DMA
+    operands = (
+        feats[0], w_conv, w_down, cotangent[0], jnp.asarray(TABLES, BF), nbr_owner, nbr_slot
+    )
     pooled, d_feats, sums = pl.pallas_call(
         kernel,
         out_shape=(
-            jax.ShapeDtypeStruct((4, 64, 128), BF),
-            jax.ShapeDtypeStruct((4, 512, 128), BF),
-            jax.ShapeDtypeStruct((3, 2, 16, 48, 128), BF),
+            pltpu.VMEM((4, 64, 128), BF),
+            pltpu.VMEM((4, 512, 128), BF),
+            pltpu.VMEM((3, 2, 16, 48, 128), BF),
         ),
-        in_specs=[anywhere] * 5 + [smem] * 2,
+        in_specs=[hbm] * 7,
         out_specs=(vmem, vmem, vmem),
         scratch_shapes=[
             buf(4, 512, 128), buf(27, 128, 128), buf(8, 128, 128), buf(4, 64, 128),
             buf(*TABLES.shape),
+            pltpu.SMEM((1, 4, 6), jnp.int32), pltpu.SMEM((1, 4, 6), jnp.int32),
             buf(100, 16, 512), buf(112, 16, 512),
             buf(9, 512, 256), buf(9, 256, 512),
-            buf(2, 2, 4, 64, 256, dtype=F32), buf(2, 2, 4, 64, 256),
+            buf(2, 8, 4, 16, 256, dtype=F32), buf(2, 8, 4, 16, 256),
             buf(4, 256, 256), buf(256, 128),
             buf(3, 2, 6, 128, 128, dtype=F32),
             *halo(64, 128, own=False), *halo(48, 256), *halo(64, 256),
             *halo(32, 256), *halo(48, 256), *halo(112, 128),
             buf(3, 768, 128), buf(3, 768, 128),
             buf(3, 16, 48, 128), buf(3, 16, 48, 128), buf(3, 8, 48, 128), buf(3, 48, 128),
-            dma((5,)),
-            dma((6, 2, 4)), dma((6, 2, 4)),
-            dma((3,)), dma((3,)),
-            dma((3, 16)), dma((3, 16)),
-            dma((3, 8)), dma((3, 8)),
-            dma((3, 16)), dma((3, 16)),
-            dma((3, 16)), dma((3, 16)),
+            dma((7,)),
+            dma((6, 4)), dma((6, 4)),
+            *([dma((3,))] * 10),
         ],
         compiler_params=pltpu.CompilerParams(
             collective_id=0, has_side_effects=True, vmem_limit_bytes=48 * 1024 * 1024
         ),
-    )(
-        feats[0], w_conv, w_down, cotangent[0], jnp.asarray(TABLES, BF), nbr_owner, nbr_slot
-    )
-    norm_factor = 1.0 / float(lax.axis_size("rep") * lax.axis_size("space") * 4 * 512) ** 0.5
-    sums = sums.reshape(3, 12, 128, 128).astype(F32) * norm_factor
-    grad_conv = sums[:, 0:9].reshape(3, 3, 3, 128, 128).transpose(1, 0, 2, 3, 4)
-    grad_down = sums[:, 9:12].reshape(9, 128, 128)[0:8]
-    return (pooled[None], d_feats[None], grad_conv.reshape(27, 128, 128), grad_down)
+    )(*[in_hbm(one) for one in operands])
+    norm = 1.0 / float(lax.axis_size("rep") * lax.axis_size("space") * 4 * 512) ** 0.5
+    pooled, d_feats, conv, down = pl.pallas_call(
+        functools.partial(epilogue, norm),
+        out_shape=(
+            jax.ShapeDtypeStruct((4, 64, 128), BF),
+            jax.ShapeDtypeStruct((4, 512, 128), BF),
+            jax.ShapeDtypeStruct((3, 3, 3, 128, 128), F32),
+            jax.ShapeDtypeStruct((8, 128, 128), F32),
+        ),
+        in_specs=[vmem] * 3,
+        out_specs=[hbm] * 4,
+        scratch_shapes=[buf(3, 3, 3, 128, 128, dtype=F32), buf(8, 128, 128, dtype=F32), dma((6,))],
+        compiler_params=pltpu.CompilerParams(vmem_limit_bytes=24 * 1024 * 1024),
+    )(sums.reshape(3, 12, 128, 128), pooled, d_feats)
+    return (pooled[None], d_feats[None], conv.reshape(27, 128, 128), down)
 
 
 def solution(mesh):

time: 88.1 us -> 61.5 us (0.70)
  Pallas kernels: 76 us -> 60.8 us
  local copies, waits for them, and re-layouts: 10.9 us -> 0 us
    pallas_call x1 -> x2, Pallas kernels: 76 us -> 60.8 us  [the longest x1 59.1 us: per_device(): pl.pallas_call(kernel, out_shape=(pltpu.VMEM((4, 64, 128), BF), pltpu.VME...]
    unnamed x16 -> x0, local copies, waits for them, and re-layouts: 8.43 us -> none
    reshape x1 -> x0, local copies, waits for them, and re-layouts: 1.4 us -> none  [per_device(): grad_conv = sums[:, 0:9].reshape(3, 3, 3, 128, 128).transpose(1, 0, 2, 3, 4)]
    slice x3 -> x0, local copies, waits for them, and re-layouts: 1.05 us -> none  [the longest x2 0.87 us: per_device(): grad_down = sums[:, 9:12].reshape(9, 128, 128)[0:8]]
where the time goes in v2:
time: 61.5 us; the launch traced here: 61.4 us
  Pallas kernels  60.8 us (99%)
  between operations  0.64 us (1%)
    pallas_call x1, Pallas kernels, per_device(): pl.pallas_call(kernel, out_shape=(pltpu.VMEM((4, 64, 128), BF), pltpu.VME...  59.1 us
    pallas_call x1, Pallas kernels, per_device(): pl.pallas_call(functools.partial(epilogue, norm), out_shape=(jax.ShapeDty...  1.62 us

profile of v2, /device:TPU:1, one launch (start us, length us, event | category | flops | bytes accessed | tf_op | source)
XLA Modules:
  0.0 61.4 jit_solution(14414512045861195772)
XLA Ops:
  0.6 59.1 %shard_map.102 = (bf16[4,64,128]{2,1,0:T(8,128)(2,1)S(1)}, bf16[4,512,128]{2,1,0:T(8,128)(2,1)S(1)}, bf16[3,2,16,48,128]{4,3,2,1,0:T(8,128)(2,1)S(1)}) custom-call(bf16[4,512,128]{2,1,0:T(8,128)(2,1)} %bitcast.7, bf16[27,128,128]{2,1,0:T(8,128)(2,1)} %wc_h.1, bf16[8,128,128]{2,1,0:T(8,128)(2,1)} %wd_h.1, bf16[4,64,128]{2,1,0:T(8,128)(2,1)} %bitcast.8, ...), custom_call_target="tpu_custom_call" | custom-call | tf_op jit(solution)/shard_map/pallas_call | solution.py:613
  59.8 1.6 %shard_map.103 = (bf16[4,64,128]{2,1,0:T(8,128)(2,1)}, bf16[4,512,128]{2,1,0:T(8,128)(2,1)}, f32[3,3,3,128,128]{4,3,2,1,0:T(8,128)}, f32[8,128,128]{2,1,0:T(8,128)}) custom-call(bf16[3,12,128,128]{3,2,1,0:T(8,128)(2,1)S(1)} %bitcast.6, bf16[4,64,128]{2,1,0:T(8,128)(2,1)S(1)} %get-tuple-element.12.pooled, bf16[4,512,128]{2,1,0:T(8,128)(2,1)S(1)} %get-tuple-element.13.dfeats), custom_call_target="tpu_custom_call" | custom-call | tf_op jit(solution)/shard_map/pallas_call | solution.py:644

commit v3 on v2

--- a/solution.py
+++ b/solution.py
@@ -334,41 +334,24 @@
 
     lax.fori_loop(0, 4, inner, 0)
 
-    halo = halo_recv(2, copies, rz)
-    for side in range(2):
-        z = 0 if side == 0 else 9
-        out = permuted("recv_z", jnp.concatenate(halo[side], axis=0))
-        for y in range(10):
-            bf[y * 10 + z, :, 0:256] = out[16 * y : 16 * y + 16]
-            bf[y * 10 + z, :, 256:512] = out[160 + 16 * y : 160 + 16 * y + 16]
-
+    middle = [(y, z) for y in range(8) for z in range(1, 7)]
     outer = [(y, z) for y in range(8) for z in (0, 7)]
-    pre = jnp.zeros((256, 256), F32)
-    for k9 in range(9):
-        tiles = [bf[(y + k9 // 3) * 10 + z + k9 % 3] for y, z in outer]
-        pre = pre + mm(jnp.concatenate(tiles, axis=0), wf[k9])
-    grad = jnp.concatenate([gh[y % 2, z, y // 2] for y, z in outer], axis=0)
-    hidden, grad = activate(pre, grad)
-    for at, (y, z) in enumerate(outer):
-        hid[y % 2, z, y // 2] = hidden[at]
-        bg[(y + 1) * 10 + z + 1, :, 128:384] = grad[at]
-
-    for side in range(2):
-        z = 8 if side == 0 else 1
-        flat = jnp.concatenate([bg[y * 10 + z, :, 128:384] for y in range(1, 9)], axis=0)
-        faces = permuted("send_gz", flat).reshape(4, 32, 256)
-        ogz[side] = faces
-        rgz[5:9, side] = faces
-    copies = halo_send(3, 2, lambda side, b: ogz[side, b], sgz, rgz)
-
-    def grad_conv(part):
+    groups = [middle[0:16], middle[16:32], middle[32:48], outer]
+
+    def tiles(ref, group, dy, dz):
+        return jnp.concatenate([ref[(y + dy) * 10 + z + dz] for y, z in group], axis=0)
+
+    def turn(at):
+        gpt[at] = tiles(bg, groups[at], 1, 1)[:, 128:384].astype(F32).T.astype(BF)
+
+    def grad_conv(part, chosen, last):
         for dz in range(3):
             first = jnp.zeros((256, 256), F32)
             second = jnp.zeros((256, 256), F32)
-            for yq in range(4):
-                rows = window(bf, 2 * yq + part, dz, 8)
-                first = first + mm(gpt[yq], rows[:, 0:256])
-                second = second + mm(gpt[yq], rows[:, 256:512])
+            for at in chosen:
+                rows = tiles(bf, groups[at], part, dz)
+                first = first + mm(gpt[at], rows[:, 0:256])
+                second = second + mm(gpt[at], rows[:, 256:512])
             taps = (
                 first[0:128, 0:128] + first[128:256, 128:256],
                 first[0:128, 128:256] + second[128:256, 0:128],
@@ -376,7 +359,38 @@
             )
             for dx in range(3):
                 slot = dx * 3 + dz
-                dwf[part, slot // 6, slot % 6] = taps[dx].T
+                to = (part, slot // 6, slot % 6)
+                dwf[to] = (dwf[to] + taps[dx]).T if last else taps[dx]
+
+    for at in range(3):
+        turn(at)
+    for part in range(3):
+        grad_conv(part, (0, 1, 2), False)
+
+    halo = halo_recv(2, copies, rz)
+    for side in range(2):
+        z = 0 if side == 0 else 9
+        out = permuted("recv_z", jnp.concatenate(halo[side], axis=0))
+        for y in range(10):
+            bf[y * 10 + z, :, 0:256] = out[16 * y : 16 * y + 16]
+            bf[y * 10 + z, :, 256:512] = out[160 + 16 * y : 160 + 16 * y + 16]
+
+    pre = jnp.zeros((256, 256), F32)
+    for k9 in range(9):
+        pre = pre + mm(tiles(bf, outer, k9 // 3, k9 % 3), wf[k9])
+    grad = jnp.concatenate([gh[y % 2, z, y // 2] for y, z in outer], axis=0)
+    hidden, grad = activate(pre, grad)
+    for at, (y, z) in enumerate(outer):
+        hid[y % 2, z, y // 2] = hidden[at]
+        bg[(y + 1) * 10 + z + 1, :, 128:384] = grad[at]
+
+    for side in range(2):
+        z = 8 if side == 0 else 1
+        flat = jnp.concatenate([bg[y * 10 + z, :, 128:384] for y in range(1, 9)], axis=0)
+        faces = permuted("send_gz", flat).reshape(4, 32, 256)
+        ogz[side] = faces
+        rgz[5:9, side] = faces
+    copies = halo_send(3, 2, lambda side, b: ogz[side, b], sgz, rgz)
 
     def core_copy(part):
         return pltpu.make_async_remote_copy(
@@ -388,47 +402,43 @@
         s1[part] = dwf[part, 1 - core].reshape(768, 128).astype(BF)
         core_copy(part).start()
 
-    def plane_copy(part, k):
-        return pltpu.make_async_remote_copy(
-            src_ref=s2.at[part, lax.rem(plane + k, N_PLANE)], dst_ref=r2.at[part, plane],
-            send_sem=xs.at[part], recv_sem=xr.at[part],
-            device_id=in_plane(k), device_id_type=MESH,
-        )
-
-    def each(low_k, high_k, act):
+    def each(count, act):
         def body(k, carry):
             act(k)
             return carry
 
-        lax.fori_loop(low_k, high_k, body, 0)
-
-    def plane_send(part):
-        core_copy(part).wait_recv()
-        mine = dwf[part, core].reshape(768, 128) + r1[part].astype(F32)
-        s2[part] = mine.astype(BF).reshape(16, 48, 128)
-        each(1, N_PLANE, lambda k: plane_copy(part, k).start())
-        r2[part, plane] = s2[part, plane]
-
-    def z_copy(part, k):
+        lax.fori_loop(1, count, body, 0)
+
+    plane_group, z_group = (N_PLANE, plane, in_plane), (N_Z, zpos, in_z)
+    order = [(plane_group, z_group), (plane_group, z_group), (z_group, plane_group)]
+
+    def chunk(part, index):
+        size = 48 // order[part][0][0]
+        return pl.ds(index * size, size)
+
+    def scatter_copy(part, k):
+        count, mine, to = order[part][0]
         return pltpu.make_async_remote_copy(
-            src_ref=r3.at[part, zpos], dst_ref=r3.at[part, zpos],
-            send_sem=zs.at[part], recv_sem=zr.at[part],
-            device_id=in_z(k), device_id_type=MESH,
+            src_ref=s2.at[part, chunk(part, lax.rem(mine + k, count))],
+            dst_ref=r2.at[part, chunk(part, mine)],
+            send_sem=xs.at[part], recv_sem=xr.at[part],
+            device_id=to(k), device_id_type=MESH,
         )
 
-    def z_send(part):
-        all_bytes(r2.at[part, 0 : N_PLANE - 1], xr.at[part])
-        total = r2[part, 0].astype(F32)
-        for i in range(1, N_PLANE):
-            total = total + r2[part, i].astype(F32)
-        r3[part, zpos] = total.astype(BF)
-        each(1, N_Z, lambda k: z_copy(part, k).start())
+    def sum_copy(part, k):
+        _, mine, to = order[part][1]
+        block = r3.at[part, chunk(part, mine)]
+        return pltpu.make_async_remote_copy(
+            src_ref=block, dst_ref=block, send_sem=zs.at[part], recv_sem=zr.at[part],
+            device_id=to(k), device_id_type=MESH,
+        )
 
     def gather_copy(part, k):
+        _, mine, to = order[part][0]
         return pltpu.make_async_remote_copy(
-            src_ref=fin.at[part], dst_ref=sums_o.at[part, core, plane],
+            src_ref=fin.at[part, chunk(part, 0)], dst_ref=sums_o.at[part, core, chunk(part, mine)],
             send_sem=as_.at[part], recv_sem=ar.at[part],
-            device_id=in_plane(k), device_id_type=MESH,
+            device_id=to(k), device_id_type=MESH,
         )
 
     def hand_copy(part):
@@ -441,33 +451,54 @@
     def all_bytes(ref, sem):
         pltpu.make_async_copy(ref, ref, sem).wait()
 
+    def sent_bytes(part, stage):
+        size = 48 // order[part][0][0]
+        return pl.ds(0, size * (order[part][stage][0] - 1))
+
+    def added(ref, part, count):
+        total = ref[part, chunk(part, 0)].astype(F32)
+        for i in range(1, count):
+            total = total + ref[part, chunk(part, i)].astype(F32)
+        return total.astype(BF)
+
+    def scatter_send(part):
+        core_copy(part).wait_recv()
+        mine = dwf[part, core].reshape(768, 128) + r1[part].astype(F32)
+        s2[part] = mine.astype(BF).reshape(48, 16, 128)
+        count, index, _ = order[part][0]
+        each(count, lambda k: scatter_copy(part, k).start())
+        r2[part, chunk(part, index)] = s2[part, chunk(part, index)]
+
+    def sum_send(part):
+        all_bytes(r2.at[part, sent_bytes(part, 0)], xr.at[part])
+        count, index, _ = order[part][1]
+        r3[part, chunk(part, index)] = added(r2, part, order[part][0][0])
+        each(count, lambda k: sum_copy(part, k).start())
+
     def gather_send(part):
-        all_bytes(r3.at[part, 0 : N_Z - 1], zr.at[part])
-        total = r3[part, 0].astype(F32)
-        for i in range(1, N_Z):
-            total = total + r3[part, i].astype(F32)
-        fin[part] = total.astype(BF)
-        each(1, N_PLANE, lambda k: gather_copy(part, k).start())
-        sums_o[part, core, plane] = fin[part]
+        all_bytes(r3.at[part, sent_bytes(part, 1)], zr.at[part])
+        count, index, _ = order[part][0]
+        total = added(r3, part, order[part][1][0])
+        fin[part, chunk(part, 0)] = total
+        each(count, lambda k: gather_copy(part, k).start())
+        sums_o[part, core, chunk(part, index)] = total
 
     def hand_over(part):
-        all_bytes(sums_o.at[part, core, 0 : N_PLANE - 1], ar.at[part])
+        all_bytes(sums_o.at[part, core, sent_bytes(part, 0)], ar.at[part])
         hand_copy(part).start()
 
     def finish(part):
         hand_copy(part).wait_recv()
         core_copy(part).wait_send()
-        all_bytes(s2.at[part, 0 : N_PLANE - 1], xs.at[part])
-        all_bytes(r3.at[part, 0 : N_Z - 1], zs.at[part])
-        all_bytes(sums_o.at[part, core, 0 : N_PLANE - 1], as_.at[part])
+        all_bytes(s2.at[part, sent_bytes(part, 0)], xs.at[part])
+        all_bytes(r3.at[part, sent_bytes(part, 1)], zs.at[part])
+        all_bytes(sums_o.at[part, core, sent_bytes(part, 0)], as_.at[part])
         hand_copy(part).wait_send()
 
     def down_rows(j, k):
         tiles = [hid[j, 2 * zq + k, yq] for yq in range(4) for zq in range(4)]
         return jnp.concatenate(tiles, axis=0)
 
-    for yq in range(4):
-        gpt[yq] = window(bg, 2 * yq + 1, 1, 8)[:, 128:384].astype(F32).T.astype(BF)
     cot_t = cotp[...].astype(F32).T.astype(BF)
     for j in range(2):
         for k in range(2):
@@ -475,11 +506,12 @@
             for i in range(2):
                 tap = 4 * i + 2 * j + k
                 dwf[tap // 3, 1, 3 + tap % 3] = out[:, 128 * i : 128 * i + 128].T
-    grad_conv(0)
-    core_send(0)
-    grad_conv(1)
-    core_send(1)
-    plane_send(0)
+    turn(3)
+    for part in range(3):
+        grad_conv(part, (3,), True)
+        core_send(part)
+    for part in range(3):
+        scatter_send(part)
 
     halo = halo_recv(2, copies, rgz)
     for side in range(2):
@@ -496,10 +528,17 @@
         ogy[side] = faces
         rgy[5:9, side] = faces
     copies = halo_send(4, 1, lambda side, b: ogy[side, b], sgy, rgy)
-    grad_conv(2)
-    core_send(2)
-    plane_send(1)
-    plane_send(2)
+    total = jnp.zeros((256, 128), F32)
+    for j in range(2):
+        for k in range(2):
+            total = total + mm(down_rows(j, k), down_weight(j, k))
+    out = permuted("swap", total.astype(BF))
+    for b in range(4):
+        for xq in range(4):
+            at = 16 * (4 * xq + b)
+            pooled_o[b, 16 * xq : 16 * xq + 16, :] = out[at : at + 16]
+    for part in range(3):
+        sum_send(part)
     halo = halo_recv(1, copies, rgy)
     for side in range(2):
         y = 0 if side == 0 else 9
@@ -507,8 +546,8 @@
         put_rows(bg, y, 0, 10, slice(128, 384), out.reshape(10, 16, 256))
 
     for group in range(7):
-        tiles = bg[16 * group : 16 * group + 16, :, 128:384].reshape(256, 256)
-        out = permuted("send_gx", tiles)
+        inside = bg[16 * group : 16 * group + 16, :, 128:384].reshape(256, 256)
+        out = permuted("send_gx", inside)
         for b in range(4):
             rows = slice(16 * group, 16 * group + 16)
             for side in range(2):
@@ -519,21 +558,11 @@
     copies = halo_send(5, 0, lambda side, b: ogx[side, b], sgx, rgx)
     for group in range(7):
         at = slice(16 * group, 16 * group + 16)
-        tiles = bg[at, :, 128:384].reshape(256, 256)
-        bg[at, :, 0:128] = permuted("low", tiles[:, 128:256]).reshape(16, 16, 128)
-        bg[at, :, 384:512] = permuted("high", tiles[:, 0:128]).reshape(16, 16, 128)
-    z_send(0)
-
-    total = jnp.zeros((256, 128), F32)
-    for j in range(2):
-        for k in range(2):
-            total = total + mm(down_rows(j, k), down_weight(j, k))
-    out = permuted("swap", total.astype(BF))
-    for b in range(4):
-        for xq in range(4):
-            at = 16 * (4 * xq + b)
-            pooled_o[b, 16 * xq : 16 * xq + 16, :] = out[at : at + 16]
-
+        inside = bg[at, :, 128:384].reshape(256, 256)
+        bg[at, :, 0:128] = permuted("low", inside[:, 128:256]).reshape(16, 16, 128)
+        bg[at, :, 384:512] = permuted("high", inside[:, 0:128]).reshape(16, 16, 128)
+    gather_send(0)
+    gather_send(1)
     halo = halo_recv(0, copies, rgx)
     for group in range(7):
         at = slice(16 * group, 16 * group + 16)
@@ -541,9 +570,6 @@
         out = permuted("insert", rows)
         bg[at, :, 0:128] = bg[at, :, 0:128] + out[0:256].reshape(16, 16, 128)
         bg[at, :, 384:512] = bg[at, :, 384:512] + out[256:512].reshape(16, 16, 128)
-
-    z_send(1)
-    z_send(2)
 
     def backward(yq, carry):
         grad = jnp.zeros((256, 256), F32)
@@ -558,14 +584,10 @@
                     dfeats_o[b, at, :] = tile[:, 128 * xl : 128 * xl + 128]
         return carry
 
-    lax.fori_loop(0, 2, backward, 0)
-    gather_send(0)
-    gather_send(1)
     gather_send(2)
-    lax.fori_loop(2, 4, backward, 0)
-    hand_over(0)
-    hand_over(1)
-    hand_over(2)
+    lax.fori_loop(0, 4, backward, 0)
+    for part in range(3):
+        hand_over(part)
     for one in sent:
         one.wait_send()
     for part in range(3):
@@ -615,7 +637,7 @@
         out_shape=(
             pltpu.VMEM((4, 64, 128), BF),
             pltpu.VMEM((4, 512, 128), BF),
-            pltpu.VMEM((3, 2, 16, 48, 128), BF),
+            pltpu.VMEM((3, 2, 48, 16, 128), BF),
         ),
         in_specs=[hbm] * 7,
         out_specs=(vmem, vmem, vmem),
@@ -631,7 +653,7 @@
             *halo(64, 128, own=False), *halo(48, 256), *halo(64, 256),
             *halo(32, 256), *halo(48, 256), *halo(112, 128),
             buf(3, 768, 128), buf(3, 768, 128),
-            buf(3, 16, 48, 128), buf(3, 16, 48, 128), buf(3, 8, 48, 128), buf(3, 48, 128),
+            buf(3, 48, 16, 128), buf(3, 48, 16, 128), buf(3, 96, 16, 128), buf(3, 6, 16, 128),
             dma((7,)),
             dma((6, 4)), dma((6, 4)),
             *([dma((3,))] * 10),

time: 61.5 us -> 58.4 us (0.950)
  Pallas kernels: 60.8 us -> 57.6 us
    pallas_call x1, Pallas kernels: 59.1 us -> 56 us  [per_device(): pl.pallas_call(kernel, out_shape=(pltpu.VMEM((4, 64, 128), BF), pltpu.VME...]
where the time goes in v3:
time: 58.4 us; the launch traced here: 58.3 us
  Pallas kernels  57.6 us (99%)
  between operations  0.64 us (1%)
    pallas_call x1, Pallas kernels, per_device(): pl.pallas_call(kernel, out_shape=(pltpu.VMEM((4, 64, 128), BF), pltpu.VME...  56 us
    pallas_call x1, Pallas kernels, per_device(): pl.pallas_call(functools.partial(epilogue, norm), out_shape=(jax.ShapeDty...  1.62 us

profile of v3, /device:TPU:1, one launch (start us, length us, event | category | flops | bytes accessed | tf_op | source)
XLA Modules:
  0.0 58.3 jit_solution(6164213096068297429)
XLA Ops:
  0.6 56.0 %shard_map.102 = (bf16[4,64,128]{2,1,0:T(8,128)(2,1)S(1)}, bf16[4,512,128]{2,1,0:T(8,128)(2,1)S(1)}, bf16[3,2,48,16,128]{4,3,2,1,0:T(8,128)(2,1)S(1)}) custom-call(bf16[4,512,128]{2,1,0:T(8,128)(2,1)} %bitcast.7, bf16[27,128,128]{2,1,0:T(8,128)(2,1)} %wc_h.1, bf16[8,128,128]{2,1,0:T(8,128)(2,1)} %wd_h.1, bf16[4,64,128]{2,1,0:T(8,128)(2,1)} %bitcast.8, ...), custom_call_target="tpu_custom_call" | custom-call | tf_op jit(solution)/shard_map/pallas_call | solution.py:635
  56.6 1.6 %shard_map.103 = (bf16[4,64,128]{2,1,0:T(8,128)(2,1)}, bf16[4,512,128]{2,1,0:T(8,128)(2,1)}, f32[3,3,3,128,128]{4,3,2,1,0:T(8,128)}, f32[8,128,128]{2,1,0:T(8,128)}) custom-call(bf16[3,12,128,128]{3,2,1,0:T(8,128)(2,1)S(1)} %bitcast.6, bf16[4,64,128]{2,1,0:T(8,128)(2,1)S(1)} %get-tuple-element.12.pooled, bf16[4,512,128]{2,1,0:T(8,128)(2,1)S(1)} %get-tuple-element.13.dfeats), custom_call_target="tpu_custom_call" | custom-call | tf_op jit(solution)/shard_map/pallas_call | solution.py:666

commit v4 on v3

--- a/solution.py
+++ b/solution.py
@@ -28,9 +28,9 @@
     for p in range(16):
         for q in range(16):
             swap[p * 16 + q, q * 16 + p] = 1
-    send_y, recv_y = table("send_y", 192, 256), table("recv_y", 256, 256)
-    send_z, recv_z = table("send_z", 256, 384), table("recv_z", 320, 256)
-    send_gz, recv_gz = table("send_gz", 128, 128), table("recv_gz", 128, 128)
+    send_y, recv_y = table("send_y", 64, 256), table("recv_y", 256, 384)
+    send_z, recv_z = table("send_z", 192, 384), table("recv_z", 384, 512)
+    move, back = table("move", 128, 128), table("back", 128, 128)
     send_gy, recv_gy = table("send_gy", 192, 256), table("recv_gy", 160, 256)
     send_gx = table("send_gx", 128, 256)
     low, high = table("low", 256, 256), table("high", 256, 256)
@@ -39,21 +39,34 @@
         for xq in range(4):
             row = xq * 4 + b
             for z in range(8):
-                send_y[b * 48 + xq * 8 + z, z * 16 + row] = 1
-                recv_y[z * 16 + row, b * 64 + xq * 8 + z] = 1
-                far = (xq + 1) * 8 + z if xq < 3 else 40 + z
-                recv_y[128 + z * 16 + row, b * 64 + far] = 1
+                at = z * 16 + row
+                recv_y[at, 128 + at - 4 if xq > 0 else 256 + b * 16 + z] = 1
+                recv_y[128 + at, at + 4 if xq < 3 else 264 + b * 16 + z] = 1
+                if xq == 0:
+                    send_y[b * 16 + z, at] = 1
                 if xq == 3:
-                    send_y[b * 48 + 40 + z, 128 + z * 16 + row] = 1
-                send_gz[b * 32 + z * 4 + xq, z * 16 + row] = 1
-                recv_gz[z * 16 + row, b * 32 + z * 4 + xq] = 1
+                    send_y[b * 16 + 8 + z, 128 + at] = 1
+                move[b * 32 + z * 4 + xq, at] = 1
+                back[at, b * 32 + z * 4 + xq] = 1
             for y in range(10):
-                send_z[b * 64 + xq * 10 + y, y * 16 + row] = 1
-                recv_z[y * 16 + row, b * 64 + xq * 10 + y] = 1
-                far = (xq + 1) * 10 + y if xq < 3 else 40 + y
-                recv_z[160 + y * 16 + row, b * 64 + far] = 1
+                at = y * 16 + row
+
+                def near(s, column):
+                    if 1 <= y <= 8:
+                        return (s - 1) * 128 + (y - 1) * 16 + column * 4 + b
+                    return 276 + b * 48 + ((y > 0) * 2 + s - 1) * 4 + column
+
+                recv_z[at, near(2, xq - 1) if xq > 0 else 256 + b * 48 + y] = 1
+                recv_z[160 + at, near(1, xq + 1) if xq < 3 else 266 + b * 48 + y] = 1
+                if xq == 0:
+                    send_z[b * 48 + y, at] = 1
                 if xq == 3:
-                    send_z[b * 64 + 40 + y, 160 + y * 16 + row] = 1
+                    send_z[b * 48 + 10 + y, 160 + at] = 1
+                if y in (0, 9):
+                    for s in (1, 2):
+                        edge = 288 + 32 * s + (y > 0) * 16 + row
+                        recv_z[edge, near(s, xq)] = 1
+                        send_z[b * 48 + 20 + ((y > 0) * 2 + s - 1) * 4 + xq, edge] = 1
                 send_gy[b * 48 + y * 4 + xq, y * 16 + row] = 1
                 recv_gy[y * 16 + row, b * 64 + y * 4 + xq] = 1
             for k in range(16):
@@ -70,7 +83,7 @@
     for name, value in tables.items():
         rows, cols = value.shape
         places[name] = (start, rows, cols)
-        parts.append(np.pad(value, ((0, 0), (0, 384 - cols))))
+        parts.append(np.pad(value, ((0, 0), (0, 512 - cols))))
         start += rows
     return places, np.concatenate(parts)
 
@@ -90,7 +103,7 @@
     feats_h, wc_h, wd_h, cot_h, tab_h, own_h, slot_h,
     pooled_o, dfeats_o, sums_o,
     feats, wc, wd, cot, tab, own_s, slot_s, bf, bg, wf, wb, gh, hid, gpt, cotp, dwf,
-    sx, rx, oy, sy, ry, oz, sz, rz, ogz, sgz, rgz, ogy, sgy, rgy, ogx, sgx, rgx,
+    sx, rx, oy, sy, ry, oz, sz, rz, oyi, syi, ryi, ozi, szi, rzi, ogz, sgz, rgz, ogy, sgy, rgy, ogx, sgx, rgx,
     s1, r1, s2, r2, r3, fin,
     lsem, hs, hr, cs, cr, xs, xr, zs, zr, as_, ar, fs, fr,
 ):
@@ -161,7 +174,7 @@
         near = jnp.clip(5 + slots[b][d], 5, 8)
         return jnp.where(owners[b][d] < 0, 4, jnp.where(gap == 0, near, far))
 
-    for ref in (rx, ry, rz, rgz, rgy, rgx):
+    for ref in (rx, ry, rz, ryi, rzi, rgz, rgy, rgx):
         ref[4] = jnp.zeros(ref.shape[1:], BF)
 
     def halo_copy(phase, i, send, recv):
@@ -238,6 +251,18 @@
         for j in range(2):
             put_rows(bf, 2 * chunk + j + 1, 1, 8, slice(128, 384), out[j])
 
+    def inner_faces(at, own, recv):
+        for side in range(2):
+            flat = jnp.concatenate([bf[i, :, 128:384] for i in at(side)], axis=0)
+            faces = permuted("move", flat).reshape(4, 32, 256)
+            own[side] = faces
+            recv[5:9, side] = faces
+
+    inner_faces(lambda side: [(8 - 7 * side) * 10 + z for z in range(1, 9)], oyi, ryi)
+    copies_y = halo_send(6, 1, lambda side, b: oyi[side, b], syi, ryi)
+    inner_faces(lambda side: [y * 10 + 8 - 7 * side for y in range(1, 9)], ozi, rzi)
+    copies_z = halo_send(7, 2, lambda side, b: ozi[side, b], szi, rzi)
+
     halo = halo_recv(0, copies, rx)
     for chunk in range(4):
         both = jnp.concatenate([x_layer(0, chunk, halo), x_layer(3, chunk, halo)], axis=1)
@@ -246,13 +271,21 @@
             put_rows(bf, 2 * chunk + j + 1, 1, 8, slice(0, 128), out[j, :, :, 0:128])
             put_rows(bf, 2 * chunk + j + 1, 1, 8, slice(384, 512), out[j, :, :, 128:256])
 
-    for side in range(2):
-        y = 8 if side == 0 else 1
-        layer = bf[y * 10 + 1 : y * 10 + 9].reshape(128, 512)
-        flat = jnp.concatenate([layer[:, 0:256], layer[:, 256:512]], axis=0)
-        faces = permuted("send_y", flat).reshape(4, 48, 256)
-        oy[side] = faces
-        ry[5:9, side] = faces
+    def both_sides(make):
+        return jnp.concatenate([make(0), make(1)], axis=1)
+
+    def y_rows(side):
+        at = (8 - 7 * side) * 10
+        low, high = bf[at + 1 : at + 9, :, 0:128], bf[at + 1 : at + 9, :, 384:512]
+        return jnp.concatenate([low.reshape(128, 128), high.reshape(128, 128)], axis=0)
+
+    def rim_faces(name, rows, count, own, recv):
+        out = permuted(name, both_sides(rows)).reshape(4, count, 256)
+        for side in range(2):
+            own[side] = out[:, :, 128 * side : 128 * side + 128]
+            recv[5:9, side] = out[:, :, 128 * side : 128 * side + 128]
+
+    rim_faces("send_y", y_rows, 16, oy, ry)
     copies = halo_send(1, 1, lambda side, b: oy[side, b], sy, ry)
 
     for one in loads[4:]:
@@ -292,22 +325,41 @@
         pad = jnp.zeros((rows - values[0].shape[0], values[0].shape[1]), BF)
         return jnp.concatenate([v for value in values for v in (value, pad)], axis=0)
 
+    def inner_halo(axis, copies, recv):
+        halo = halo_recv(axis, copies, recv)
+        return [permuted("back", jnp.concatenate(halo[side], axis=0)) for side in range(2)]
+
+    def rim_rows(inside, halo, rows):
+        def one(side):
+            pad = jnp.zeros((rows - 256 - 4 * halo[side][0].shape[0], 128), BF)
+            parts = [inside[side][:, 0:128], inside[side][:, 128:256], *halo[side], pad]
+            return jnp.concatenate(parts, axis=0)
+
+        return both_sides(one)
+
+    inside = inner_halo(1, copies_y, ryi)
+    for side in range(2):
+        put_rows(bf, 9 * side, 1, 8, slice(128, 384), inside[side].reshape(8, 16, 256))
     halo = halo_recv(1, copies, ry)
-    for side in range(2):
-        y = 0 if side == 0 else 9
-        out = permuted("recv_y", tall(halo[side], 64))
-        put_rows(bf, y, 1, 8, slice(0, 256), out[0:128].reshape(8, 16, 256))
-        put_rows(bf, y, 1, 8, slice(256, 512), out[128:256].reshape(8, 16, 256))
-
-    for side in range(2):
-        z = 8 if side == 0 else 1
-        near = [bf[y * 10 + z, :, 0:256] for y in range(10)]
-        far = [bf[y * 10 + z, :, 256:512] for y in range(10)]
-        flat = jnp.concatenate(near + far + [jnp.zeros((64, 256), BF)], axis=0)
-        faces = permuted("send_z", flat).reshape(4, 64, 256)
-        oz[side] = faces
-        rz[5:9, side] = faces
+    out = permuted("recv_y", rim_rows(inside, halo, 384)).reshape(2, 8, 16, 256)
+    for side in range(2):
+        lanes = slice(128 * side, 128 * side + 128)
+        put_rows(bf, 9 * side, 1, 8, slice(0, 128), out[0, :, :, lanes])
+        put_rows(bf, 9 * side, 1, 8, slice(384, 512), out[1, :, :, lanes])
+
+    def z_rows(side):
+        at = 8 - 7 * side
+        parts = [bf[y * 10 + at, :, 0:128] for y in range(10)]
+        parts += [bf[y * 10 + at, :, 384:512] for y in range(10)]
+        parts += [bf[y * 10 + at, :, 128 * s : 128 * s + 128] for s in (1, 2) for y in (0, 9)]
+        return jnp.concatenate(parts, axis=0)
+
+    rim_faces("send_z", z_rows, 48, oz, rz)
     copies = halo_send(2, 2, lambda side, b: oz[side, b], sz, rz)
+    inside = inner_halo(2, copies_z, rzi)
+    for side in range(2):
+        for y in range(1, 9):
+            bf[y * 10 + 9 * side, :, 128:384] = inside[side][16 * y - 16 : 16 * y]
     bg[100:112] = jnp.zeros((12, 16, 512), BF)
     dwf[2, 1, 5] = jnp.zeros((128, 128), F32)
     def window(ref, y, z, count):
@@ -368,12 +420,15 @@
         grad_conv(part, (0, 1, 2), False)
 
     halo = halo_recv(2, copies, rz)
-    for side in range(2):
-        z = 0 if side == 0 else 9
-        out = permuted("recv_z", jnp.concatenate(halo[side], axis=0))
+    out = permuted("recv_z", rim_rows(inside, halo, 512)).reshape(24, 16, 256)
+    for side in range(2):
+        lanes = slice(128 * side, 128 * side + 128)
         for y in range(10):
-            bf[y * 10 + z, :, 0:256] = out[16 * y : 16 * y + 16]
-            bf[y * 10 + z, :, 256:512] = out[160 + 16 * y : 160 + 16 * y + 16]
+            bf[y * 10 + 9 * side, :, 0:128] = out[y, :, lanes]
+            bf[y * 10 + 9 * side, :, 384:512] = out[10 + y, :, lanes]
+        for i, y in enumerate((0, 9)):
+            bf[y * 10 + 9 * side, :, 128:256] = out[20 + i, :, lanes]
+            bf[y * 10 + 9 * side, :, 256:384] = out[22 + i, :, lanes]
 
     pre = jnp.zeros((256, 256), F32)
     for k9 in range(9):
@@ -387,7 +442,7 @@
     for side in range(2):
         z = 8 if side == 0 else 1
         flat = jnp.concatenate([bg[y * 10 + z, :, 128:384] for y in range(1, 9)], axis=0)
-        faces = permuted("send_gz", flat).reshape(4, 32, 256)
+        faces = permuted("move", flat).reshape(4, 32, 256)
         ogz[side] = faces
         rgz[5:9, side] = faces
     copies = halo_send(3, 2, lambda side, b: ogz[side, b], sgz, rgz)
@@ -410,7 +465,7 @@
         lax.fori_loop(1, count, body, 0)
 
     plane_group, z_group = (N_PLANE, plane, in_plane), (N_Z, zpos, in_z)
-    order = [(plane_group, z_group), (plane_group, z_group), (z_group, plane_group)]
+    order = [(plane_group, z_group)] * 3
 
     def chunk(part, index):
         size = 48 // order[part][0][0]
@@ -516,7 +571,7 @@
     halo = halo_recv(2, copies, rgz)
     for side in range(2):
         z = 0 if side == 0 else 9
-        out = permuted("recv_gz", jnp.concatenate(halo[side], axis=0))
+        out = permuted("back", jnp.concatenate(halo[side], axis=0))
         for y in range(8):
             bg[(y + 1) * 10 + z, :, 128:384] = out[16 * y : 16 * y + 16]
 
@@ -537,8 +592,8 @@
         for xq in range(4):
             at = 16 * (4 * xq + b)
             pooled_o[b, 16 * xq : 16 * xq + 16, :] = out[at : at + 16]
-    for part in range(3):
-        sum_send(part)
+    sum_send(0)
+    sum_send(1)
     halo = halo_recv(1, copies, rgy)
     for side in range(2):
         y = 0 if side == 0 else 9
@@ -561,6 +616,7 @@
         inside = bg[at, :, 128:384].reshape(256, 256)
         bg[at, :, 0:128] = permuted("low", inside[:, 128:256]).reshape(16, 16, 128)
         bg[at, :, 384:512] = permuted("high", inside[:, 0:128]).reshape(16, 16, 128)
+    sum_send(2)
     gather_send(0)
     gather_send(1)
     halo = halo_recv(0, copies, rgx)
@@ -650,12 +706,13 @@
             buf(2, 8, 4, 16, 256, dtype=F32), buf(2, 8, 4, 16, 256),
             buf(4, 256, 256), buf(256, 128),
             buf(3, 2, 6, 128, 128, dtype=F32),
-            *halo(64, 128, own=False), *halo(48, 256), *halo(64, 256),
+            *halo(64, 128, own=False), *halo(16, 128), *halo(48, 128),
+            *halo(32, 256), *halo(32, 256),
             *halo(32, 256), *halo(48, 256), *halo(112, 128),
             buf(3, 768, 128), buf(3, 768, 128),
             buf(3, 48, 16, 128), buf(3, 48, 16, 128), buf(3, 96, 16, 128), buf(3, 6, 16, 128),
             dma((7,)),
-            dma((6, 4)), dma((6, 4)),
+            dma((8, 4)), dma((8, 4)),
             *([dma((3,))] * 10),
         ],
         compiler_params=pltpu.CompilerParams(

time: 58.4 us -> 57 us (0.976)
  Pallas kernels: 57.6 us -> 56.3 us
    pallas_call x1, Pallas kernels: 56 us -> 54.6 us  [per_device(): pl.pallas_call(kernel, out_shape=(pltpu.VMEM((4, 64, 128), BF), pltpu.VME...]
where the time goes in v4:
time: 57 us; the launch traced here: 56.9 us
  Pallas kernels  56.3 us (99%)
  between operations  0.64 us (1%)
    pallas_call x1, Pallas kernels, per_device(): pl.pallas_call(kernel, out_shape=(pltpu.VMEM((4, 64, 128), BF), pltpu.VME...  54.6 us
    pallas_call x1, Pallas kernels, per_device(): pl.pallas_call(functools.partial(epilogue, norm), out_shape=(jax.ShapeDty...  1.62 us

profile of v4, /device:TPU:1, one launch (start us, length us, event | category | flops | bytes accessed | tf_op | source)
XLA Modules:
  0.0 56.9 jit_solution(3364576480550982066)
XLA Ops:
  0.6 54.6 %shard_map.102 = (bf16[4,64,128]{2,1,0:T(8,128)(2,1)S(1)}, bf16[4,512,128]{2,1,0:T(8,128)(2,1)S(1)}, bf16[3,2,48,16,128]{4,3,2,1,0:T(8,128)(2,1)S(1)}) custom-call(bf16[4,512,128]{2,1,0:T(8,128)(2,1)} %bitcast.7, bf16[27,128,128]{2,1,0:T(8,128)(2,1)} %wc_h.1, bf16[8,128,128]{2,1,0:T(8,128)(2,1)} %wd_h.1, bf16[4,64,128]{2,1,0:T(8,128)(2,1)} %bitcast.8, ...), custom_call_target="tpu_custom_call" | custom-call | tf_op jit(solution)/shard_map/pallas_call | solution.py:691
  55.3 1.6 %shard_map.103 = (bf16[4,64,128]{2,1,0:T(8,128)(2,1)}, bf16[4,512,128]{2,1,0:T(8,128)(2,1)}, f32[3,3,3,128,128]{4,3,2,1,0:T(8,128)}, f32[8,128,128]{2,1,0:T(8,128)}) custom-call(bf16[3,12,128,128]{3,2,1,0:T(8,128)(2,1)S(1)} %bitcast.6, bf16[4,64,128]{2,1,0:T(8,128)(2,1)S(1)} %get-tuple-element.12.pooled, bf16[4,512,128]{2,1,0:T(8,128)(2,1)S(1)} %get-tuple-element.13.dfeats), custom_call_target="tpu_custom_call" | custom-call | tf_op jit(solution)/shard_map/pallas_call | solution.py:723

commit v5 on v4

--- a/solution.py
+++ b/solution.py
@@ -28,10 +28,11 @@
     for p in range(16):
         for q in range(16):
             swap[p * 16 + q, q * 16 + p] = 1
-    send_y, recv_y = table("send_y", 64, 256), table("recv_y", 256, 384)
-    send_z, recv_z = table("send_z", 192, 384), table("recv_z", 384, 512)
+    send_y, recv_y = table("send_y", 128, 256), table("recv_y", 256, 384)
+    wide, recv_z = np.zeros((768, 768), np.float32), table("recv_z", 384, 512)
+    send_z, send_gr = wide[0:384], wide[384:768]
     move, back = table("move", 128, 128), table("back", 128, 128)
-    send_gy, recv_gy = table("send_gy", 192, 256), table("recv_gy", 160, 256)
+    send_gy, recv_gy = table("send_gy", 128, 512), table("recv_gy", 64, 128)
     send_gx = table("send_gx", 128, 256)
     low, high = table("low", 256, 256), table("high", 256, 256)
     insert = table("insert", 512, 128)
@@ -42,10 +43,6 @@
                 at = z * 16 + row
                 recv_y[at, 128 + at - 4 if xq > 0 else 256 + b * 16 + z] = 1
                 recv_y[128 + at, at + 4 if xq < 3 else 264 + b * 16 + z] = 1
-                if xq == 0:
-                    send_y[b * 16 + z, at] = 1
-                if xq == 3:
-                    send_y[b * 16 + 8 + z, 128 + at] = 1
                 move[b * 32 + z * 4 + xq, at] = 1
                 back[at, b * 32 + z * 4 + xq] = 1
             for y in range(10):
@@ -58,22 +55,44 @@
 
                 recv_z[at, near(2, xq - 1) if xq > 0 else 256 + b * 48 + y] = 1
                 recv_z[160 + at, near(1, xq + 1) if xq < 3 else 266 + b * 48 + y] = 1
-                if xq == 0:
-                    send_z[b * 48 + y, at] = 1
-                if xq == 3:
-                    send_z[b * 48 + 10 + y, 160 + at] = 1
                 if y in (0, 9):
                     for s in (1, 2):
                         edge = 288 + 32 * s + (y > 0) * 16 + row
                         recv_z[edge, near(s, xq)] = 1
-                        send_z[b * 48 + 20 + ((y > 0) * 2 + s - 1) * 4 + xq, edge] = 1
-                send_gy[b * 48 + y * 4 + xq, y * 16 + row] = 1
-                recv_gy[y * 16 + row, b * 64 + y * 4 + xq] = 1
+                        cell = 20 + ((y > 0) * 2 + s - 1) * 4 + xq
+                        for side in range(2):
+                            tile = 32 + (side * 2 + (y > 0)) * 2 + s - 1
+                            send_z[side * 192 + b * 48 + cell, tile * 16 + row] = 1
             for k in range(16):
                 if xq >= 1:
                     low[k * 16 + row, k * 16 + row - 4] = 1
                 if xq <= 2:
                     high[k * 16 + row, k * 16 + row + 4] = 1
+        for side in range(2):
+            for zs in range(2):
+                for xl in range(2):
+                    for xq in range(4):
+                        cell = b * 16 + zs * 8 + xl * 4 + xq
+                        at = side * 256 + ((zs * 4 + b) * 2 + xl) * 16 + 12 - 12 * side + xq
+                        send_gy[side * 64 + cell, at] = 1
+                        recv_gy[xl * 32 + zs * 16 + xq * 4 + b, cell] = 1
+            to, xq = side * 192 + b * 48, 3 - 3 * side
+            for edge in range(2):
+                for i in range(8):
+                    send_gr[to + edge * 10 + 1 + i, edge * 128 + i * 16 + xq * 4 + b] = 1
+                    send_gr[to + 20 + edge * 8 + i, 256 + edge * 128 + i * 16 + xq * 4 + b] = 1
+                for zs in range(2):
+                    at = 512 + (edge * 4 + b) * 16 + zs * 8 + 4 - 4 * side + xq
+                    send_gr[to + edge * 10 + 9 * zs, at] = 1
+            for end in range(2):
+                to = side * 192 + b * 48 + end * 10
+                for z in range(8):
+                    at = side * 128 + (end * 4 + b) * 16 + 8 - 8 * side + z
+                    send_y[side * 64 + b * 16 + end * 8 + z, at] = 1
+                    send_z[to + 1 + z, (end * 4 + b) * 64 + z * 8 + 7 - 7 * side] = 1
+                for edge in range(2):
+                    at = 640 + (edge * 4 + b) * 16 + end * 8 + 7 - 7 * side
+                    send_z[to + 9 * edge, at] = 1
         for k in range(16):
             send_gx[b * 16 + k, k * 16 + 12 + b] = 1
             send_gx[64 + b * 16 + k, k * 16 + b] = 1
@@ -85,10 +104,10 @@
         places[name] = (start, rows, cols)
         parts.append(np.pad(value, ((0, 0), (0, 512 - cols))))
         start += rows
-    return places, np.concatenate(parts)
-
-
-PLACES, TABLES = onehot_tables()
+    return places, np.concatenate(parts), wide
+
+
+PLACES, TABLES, WIDE = onehot_tables()
 
 
 def mm(left, right):
@@ -100,12 +119,13 @@
 
 
 def kernel(
-    feats_h, wc_h, wd_h, cot_h, tab_h, own_h, slot_h,
+    feats_h, wc_h, wd_h, cot_h, tab_h, wide_h, own_h, slot_h,
     pooled_o, dfeats_o, sums_o,
-    feats, wc, wd, cot, tab, own_s, slot_s, bf, bg, wf, wb, gh, hid, gpt, cotp, dwf,
+    feats, wc, wd, cot, tab, wide, own_s, slot_s, bf, bg, wf, wb, gh, hid, gpt, cotp, dwf,
     sx, rx, oy, sy, ry, oz, sz, rz, oyi, syi, ryi, ozi, szi, rzi, ogz, sgz, rgz, ogy, sgy, rgy, ogx, sgx, rgx,
+    ogyi, sgyi, rgyi, ogxi, sgxi, rgxi,
     s1, r1, s2, r2, r3, fin,
-    lsem, hs, hr, cs, cr, xs, xr, zs, zr, as_, ar, fs, fr,
+    lsem, hs, hr, cs, cr, xs, xr, vs, vr, as_, ar, fs, fr,
 ):
     pos = lax.axis_index("space")
     rep = lax.axis_index("rep")
@@ -131,7 +151,7 @@
         for i, (src, dst) in enumerate(
             (
                 (own_h, own_s), (slot_h, slot_s), (feats_h, feats), (tab_h, tab),
-                (cot_h, cot), (wc_h, wc), (wd_h, wd),
+                (cot_h, cot), (wc_h, wc), (wd_h, wd), (wide_h, wide),
             )
         )
     ]
@@ -174,7 +194,7 @@
         near = jnp.clip(5 + slots[b][d], 5, 8)
         return jnp.where(owners[b][d] < 0, 4, jnp.where(gap == 0, near, far))
 
-    for ref in (rx, ry, rz, ryi, rzi, rgz, rgy, rgx):
+    for ref in (rx, ry, rz, ryi, rzi, rgz, rgy, rgx, rgyi, rgxi):
         ref[4] = jnp.zeros(ref.shape[1:], BF)
 
     def halo_copy(phase, i, send, recv):
@@ -251,42 +271,37 @@
         for j in range(2):
             put_rows(bf, 2 * chunk + j + 1, 1, 8, slice(128, 384), out[j])
 
-    def inner_faces(at, own, recv):
+    def inner_faces(ref, at, own, recv):
         for side in range(2):
-            flat = jnp.concatenate([bf[i, :, 128:384] for i in at(side)], axis=0)
+            flat = jnp.concatenate([ref[i, :, 128:384] for i in at(side)], axis=0)
             faces = permuted("move", flat).reshape(4, 32, 256)
             own[side] = faces
             recv[5:9, side] = faces
 
-    inner_faces(lambda side: [(8 - 7 * side) * 10 + z for z in range(1, 9)], oyi, ryi)
+    inner_faces(bf, lambda side: [(8 - 7 * side) * 10 + z for z in range(1, 9)], oyi, ryi)
     copies_y = halo_send(6, 1, lambda side, b: oyi[side, b], syi, ryi)
-    inner_faces(lambda side: [y * 10 + 8 - 7 * side for y in range(1, 9)], ozi, rzi)
+    inner_faces(bf, lambda side: [y * 10 + 8 - 7 * side for y in range(1, 9)], ozi, rzi)
     copies_z = halo_send(7, 2, lambda side, b: ozi[side, b], szi, rzi)
 
     halo = halo_recv(0, copies, rx)
+    def rim_faces(out, count, own, recv):
+        faces = out.astype(BF).reshape(2, 4, count, 128)
+        for side in range(2):
+            own[side] = faces[side]
+            recv[5:9, side] = faces[side]
+
+    ends = [[halo[end][b][rows] for end in range(2) for b in range(4)]
+            for rows in (slice(48, 64), slice(0, 16))]
+    rim_faces(mm(onehot("send_y"), jnp.concatenate(ends[0] + ends[1], axis=0)), 16, oy, ry)
+    copies = halo_send(1, 1, lambda side, b: oy[side, b], sy, ry)
+    x_halo = [halo[end][b] for end in range(2) for b in range(4)]
+
     for chunk in range(4):
         both = jnp.concatenate([x_layer(0, chunk, halo), x_layer(3, chunk, halo)], axis=1)
         out = permuted("swap", both).reshape(2, 8, 16, 256)
         for j in range(2):
             put_rows(bf, 2 * chunk + j + 1, 1, 8, slice(0, 128), out[j, :, :, 0:128])
             put_rows(bf, 2 * chunk + j + 1, 1, 8, slice(384, 512), out[j, :, :, 128:256])
-
-    def both_sides(make):
-        return jnp.concatenate([make(0), make(1)], axis=1)
-
-    def y_rows(side):
-        at = (8 - 7 * side) * 10
-        low, high = bf[at + 1 : at + 9, :, 0:128], bf[at + 1 : at + 9, :, 384:512]
-        return jnp.concatenate([low.reshape(128, 128), high.reshape(128, 128)], axis=0)
-
-    def rim_faces(name, rows, count, own, recv):
-        out = permuted(name, both_sides(rows)).reshape(4, count, 256)
-        for side in range(2):
-            own[side] = out[:, :, 128 * side : 128 * side + 128]
-            recv[5:9, side] = out[:, :, 128 * side : 128 * side + 128]
-
-    rim_faces("send_y", y_rows, 16, oy, ry)
-    copies = halo_send(1, 1, lambda side, b: oy[side, b], sy, ry)
 
     for one in loads[4:]:
         one.wait()
@@ -321,9 +336,8 @@
 
     lax.fori_loop(0, 9, weights, 0)
 
-    def tall(values, rows):
-        pad = jnp.zeros((rows - values[0].shape[0], values[0].shape[1]), BF)
-        return jnp.concatenate([v for value in values for v in (value, pad)], axis=0)
+    def both_sides(make):
+        return jnp.concatenate([make(0), make(1)], axis=1)
 
     def inner_halo(axis, copies, recv):
         halo = halo_recv(axis, copies, recv)
@@ -340,22 +354,22 @@
     inside = inner_halo(1, copies_y, ryi)
     for side in range(2):
         put_rows(bf, 9 * side, 1, 8, slice(128, 384), inside[side].reshape(8, 16, 256))
+    corner_tiles = [
+        inside[edge][16 * z : 16 * z + 16, 128 * s : 128 * s + 128]
+        for z in (7, 0) for edge in range(2) for s in range(2)
+    ]
+    early = mm(wide[0:384, 0:640], jnp.concatenate(x_halo + corner_tiles, axis=0))
     halo = halo_recv(1, copies, ry)
+
+    late = jnp.concatenate([halo[side][b] for side in range(2) for b in range(4)], axis=0)
+    rim_faces(early + mm(wide[0:384, 640:768], late), 48, oz, rz)
+    copies = halo_send(2, 2, lambda side, b: oz[side, b], sz, rz)
     out = permuted("recv_y", rim_rows(inside, halo, 384)).reshape(2, 8, 16, 256)
     for side in range(2):
         lanes = slice(128 * side, 128 * side + 128)
         put_rows(bf, 9 * side, 1, 8, slice(0, 128), out[0, :, :, lanes])
         put_rows(bf, 9 * side, 1, 8, slice(384, 512), out[1, :, :, lanes])
 
-    def z_rows(side):
-        at = 8 - 7 * side
-        parts = [bf[y * 10 + at, :, 0:128] for y in range(10)]
-        parts += [bf[y * 10 + at, :, 384:512] for y in range(10)]
-        parts += [bf[y * 10 + at, :, 128 * s : 128 * s + 128] for s in (1, 2) for y in (0, 9)]
-        return jnp.concatenate(parts, axis=0)
-
-    rim_faces("send_z", z_rows, 48, oz, rz)
-    copies = halo_send(2, 2, lambda side, b: oz[side, b], sz, rz)
     inside = inner_halo(2, copies_z, rzi)
     for side in range(2):
         for y in range(1, 9):
@@ -484,7 +498,7 @@
         _, mine, to = order[part][1]
         block = r3.at[part, chunk(part, mine)]
         return pltpu.make_async_remote_copy(
-            src_ref=block, dst_ref=block, send_sem=zs.at[part], recv_sem=zr.at[part],
+            src_ref=block, dst_ref=block, send_sem=vs.at[part], recv_sem=vr.at[part],
             device_id=to(k), device_id_type=MESH,
         )
 
@@ -531,7 +545,7 @@
         each(count, lambda k: sum_copy(part, k).start())
 
     def gather_send(part):
-        all_bytes(r3.at[part, sent_bytes(part, 1)], zr.at[part])
+        all_bytes(r3.at[part, sent_bytes(part, 1)], vr.at[part])
         count, index, _ = order[part][0]
         total = added(r3, part, order[part][1][0])
         fin[part, chunk(part, 0)] = total
@@ -546,7 +560,7 @@
         hand_copy(part).wait_recv()
         core_copy(part).wait_send()
         all_bytes(s2.at[part, sent_bytes(part, 0)], xs.at[part])
-        all_bytes(r3.at[part, sent_bytes(part, 1)], zs.at[part])
+        all_bytes(r3.at[part, sent_bytes(part, 1)], vs.at[part])
         all_bytes(sums_o.at[part, core, sent_bytes(part, 0)], as_.at[part])
         hand_copy(part).wait_send()
 
@@ -565,24 +579,63 @@
     for part in range(3):
         grad_conv(part, (3,), True)
         core_send(part)
+
+    inner_faces(bg, lambda side: [(8 - 7 * side) * 10 + z for z in range(1, 9)], ogyi, rgyi)
+    copies_y = halo_send(8, 1, lambda side, b: ogyi[side, b], sgyi, rgyi)
+    within = [y * 10 + z for y in range(1, 9) for z in range(1, 9)]
+    rim = [*range(0, 10), *range(90, 100), *range(10, 90, 10), *range(19, 90, 10)]
+    rim += list(range(100, 112))
+
+    def inside_rows(group):
+        return jnp.concatenate([bg[i, :, 128:384] for i in group], axis=0)
+
+    for group in range(4):
+        rows = slice(16 * group, 16 * group + 16)
+        out = permuted("send_gx", inside_rows(within[rows]))
+        for b in range(4):
+            for side in range(2):
+                lanes = slice(128, 256) if side == 0 else slice(0, 128)
+                face = out[64 * side + 16 * b : 64 * side + 16 * b + 16, lanes]
+                ogxi[side, b, rows] = face
+                rgxi[5 + b, side, rows] = face
+    copies_x = halo_send(9, 0, lambda side, b: ogxi[side, b], sgxi, rgxi)
+
     for part in range(3):
         scatter_send(part)
 
     halo = halo_recv(2, copies, rgz)
+    ends = [
+        halo[zs][b][rows, 128 * xl : 128 * xl + 128]
+        for rows in (slice(16, 32), slice(0, 16))
+        for zs in range(2) for b in range(4) for xl in range(2)
+    ]
+    rim_faces(mm(onehot("send_gy"), jnp.concatenate(ends, axis=0)), 16, ogy, rgy)
+    copies = halo_send(4, 1, lambda side, b: ogy[side, b], sgy, rgy)
+    inside_z = [permuted("back", jnp.concatenate(halo[zs], axis=0)) for zs in range(2)]
+    inside_y = inner_halo(1, copies_y, rgyi)
     for side in range(2):
-        z = 0 if side == 0 else 9
-        out = permuted("back", jnp.concatenate(halo[side], axis=0))
-        for y in range(8):
-            bg[(y + 1) * 10 + z, :, 128:384] = out[16 * y : 16 * y + 16]
-
-    for side in range(2):
-        y = 8 if side == 0 else 1
-        flat = bg[y * 10 : y * 10 + 10, :, 128:384].reshape(160, 256)
-        flat = jnp.concatenate([flat, jnp.zeros((96, 256), BF)], axis=0)
-        faces = permuted("send_gy", flat).reshape(4, 48, 256)
-        ogy[side] = faces
-        rgy[5:9, side] = faces
-    copies = halo_send(4, 1, lambda side, b: ogy[side, b], sgy, rgy)
+        for y in range(1, 9):
+            bg[y * 10 + 9 * side, :, 128:384] = inside_z[side][16 * y - 16 : 16 * y]
+        put_rows(bg, 9 * side, 1, 8, slice(128, 384), inside_y[side].reshape(8, 16, 256))
+    early = mm(wide[384:768, 0:512], jnp.concatenate(inside_y + inside_z, axis=0))
+
+    def shift_rows(group):
+        rows = inside_rows(group)
+        lower = permuted("low", rows[:, 128:256]).reshape(16, 16, 128)
+        upper = permuted("high", rows[:, 0:128]).reshape(16, 16, 128)
+        for at, i in enumerate(group):
+            bg[i, :, 0:128] = lower[at]
+            bg[i, :, 384:512] = upper[at]
+
+    def insert_rows(group, halo, rows):
+        layers = [halo[side][b][rows] for side in range(2) for b in range(4)]
+        out = permuted("insert", jnp.concatenate(layers, axis=0)).reshape(32, 16, 128)
+        for at, i in enumerate(group):
+            bg[i, :, 0:128] = bg[i, :, 0:128] + out[at]
+            bg[i, :, 384:512] = bg[i, :, 384:512] + out[16 + at]
+
+    for group in range(4):
+        shift_rows(within[16 * group : 16 * group + 16])
     total = jnp.zeros((256, 128), F32)
     for j in range(2):
         for k in range(2):
@@ -595,37 +648,33 @@
     sum_send(0)
     sum_send(1)
     halo = halo_recv(1, copies, rgy)
+    late = jnp.concatenate([halo[side][b] for side in range(2) for b in range(4)], axis=0)
+    late = mm(wide[384:768, 512:640], late)
+    faces = (early[0:192, 128:256] + late[0:192], early[192:384, 0:128] + late[192:384])
+    rim_faces(jnp.concatenate(faces, axis=0), 48, ogx, rgx)
+    copies = halo_send(5, 0, lambda side, b: ogx[side, b], sgx, rgx)
+    corners = both_sides(lambda side: jnp.concatenate(halo[side], axis=0))
+    corners = jnp.concatenate([corners, jnp.zeros((64, 256), BF)], axis=0)
+    out = permuted("recv_gy", corners).reshape(2, 2, 16, 256)
     for side in range(2):
-        y = 0 if side == 0 else 9
-        out = permuted("recv_gy", tall(halo[side], 64))
-        put_rows(bg, y, 0, 10, slice(128, 384), out.reshape(10, 16, 256))
-
-    for group in range(7):
-        inside = bg[16 * group : 16 * group + 16, :, 128:384].reshape(256, 256)
-        out = permuted("send_gx", inside)
-        for b in range(4):
-            rows = slice(16 * group, 16 * group + 16)
-            for side in range(2):
-                lanes = slice(128, 256) if side == 0 else slice(0, 128)
-                face = out[64 * side + 16 * b : 64 * side + 16 * b + 16, lanes]
-                ogx[side, b, rows] = face
-                rgx[5 + b, side, rows] = face
-    copies = halo_send(5, 0, lambda side, b: ogx[side, b], sgx, rgx)
-    for group in range(7):
-        at = slice(16 * group, 16 * group + 16)
-        inside = bg[at, :, 128:384].reshape(256, 256)
-        bg[at, :, 0:128] = permuted("low", inside[:, 128:256]).reshape(16, 16, 128)
-        bg[at, :, 384:512] = permuted("high", inside[:, 0:128]).reshape(16, 16, 128)
+        for zs in range(2):
+            for xl in range(2):
+                lanes = slice(128 + 128 * xl, 256 + 128 * xl)
+                face = out[xl, zs, :, 128 * side : 128 * side + 128]
+                bg[90 * side + 9 * zs, :, lanes] = face
+    for group in range(3):
+        shift_rows(rim[16 * group : 16 * group + 16])
     sum_send(2)
+    halo = halo_recv(0, copies_x, rgxi)
+    for group in range(4):
+        rows = slice(16 * group, 16 * group + 16)
+        insert_rows(within[rows], halo, rows)
     gather_send(0)
     gather_send(1)
     halo = halo_recv(0, copies, rgx)
-    for group in range(7):
-        at = slice(16 * group, 16 * group + 16)
-        rows = jnp.concatenate([halo[side][b][at] for side in range(2) for b in range(4)], axis=0)
-        out = permuted("insert", rows)
-        bg[at, :, 0:128] = bg[at, :, 0:128] + out[0:256].reshape(16, 16, 128)
-        bg[at, :, 384:512] = bg[at, :, 384:512] + out[256:512].reshape(16, 16, 128)
+    for group in range(3):
+        rows = slice(16 * group, 16 * group + 16)
+        insert_rows(rim[rows], halo, rows)
 
     def backward(yq, carry):
         grad = jnp.zeros((256, 256), F32)
@@ -686,7 +735,8 @@
     hbm = pl.BlockSpec(memory_space=pltpu.HBM)
     dma = pltpu.SemaphoreType.DMA
     operands = (
-        feats[0], w_conv, w_down, cotangent[0], jnp.asarray(TABLES, BF), nbr_owner, nbr_slot
+        feats[0], w_conv, w_down, cotangent[0], jnp.asarray(TABLES, BF), jnp.asarray(WIDE, BF),
+        nbr_owner, nbr_slot,
     )
     pooled, d_feats, sums = pl.pallas_call(
         kernel,
@@ -695,11 +745,11 @@
             pltpu.VMEM((4, 512, 128), BF),
             pltpu.VMEM((3, 2, 48, 16, 128), BF),
         ),
-        in_specs=[hbm] * 7,
+        in_specs=[hbm] * 8,
         out_specs=(vmem, vmem, vmem),
         scratch_shapes=[
             buf(4, 512, 128), buf(27, 128, 128), buf(8, 128, 128), buf(4, 64, 128),
-            buf(*TABLES.shape),
+            buf(*TABLES.shape), buf(*WIDE.shape),
             pltpu.SMEM((1, 4, 6), jnp.int32), pltpu.SMEM((1, 4, 6), jnp.int32),
             buf(100, 16, 512), buf(112, 16, 512),
             buf(9, 512, 256), buf(9, 256, 512),
@@ -708,11 +758,12 @@
             buf(3, 2, 6, 128, 128, dtype=F32),
             *halo(64, 128, own=False), *halo(16, 128), *halo(48, 128),
             *halo(32, 256), *halo(32, 256),
-            *halo(32, 256), *halo(48, 256), *halo(112, 128),
+            *halo(32, 256), *halo(16, 128), *halo(48, 128),
+            *halo(32, 256), *halo(64, 128),
             buf(3, 768, 128), buf(3, 768, 128),
             buf(3, 48, 16, 128), buf(3, 48, 16, 128), buf(3, 96, 16, 128), buf(3, 6, 16, 128),
-            dma((7,)),
-            dma((8, 4)), dma((8, 4)),
+            dma((8,)),
+            dma((10, 4)), dma((10, 4)),
             *([dma((3,))] * 10),
         ],
         compiler_params=pltpu.CompilerParams(

time: 57 us -> 56.6 us (level)
  no operation moved by 1% of the time
where the time goes in v5:
time: 56.6 us; the launch traced here: 56.5 us
  Pallas kernels  55.9 us (99%)
  between operations  0.64 us (1%)
    pallas_call x1, Pallas kernels, per_device(): pl.pallas_call(kernel, out_shape=(pltpu.VMEM((4, 64, 128), BF), pltpu.VME...  54.3 us
    pallas_call x1, Pallas kernels, per_device(): pl.pallas_call(functools.partial(epilogue, norm), out_shape=(jax.ShapeDty...  1.62 us

profile of v5, /device:TPU:1, one launch (start us, length us, event | category | flops | bytes accessed | tf_op | source)
XLA Modules:
  0.0 56.5 jit_solution(17663544325464743011)
XLA Ops:
  0.6 54.3 %shard_map.111 = (bf16[4,64,128]{2,1,0:T(8,128)(2,1)S(1)}, bf16[4,512,128]{2,1,0:T(8,128)(2,1)S(1)}, bf16[3,2,48,16,128]{4,3,2,1,0:T(8,128)(2,1)S(1)}) custom-call(bf16[4,512,128]{2,1,0:T(8,128)(2,1)} %bitcast.7, bf16[27,128,128]{2,1,0:T(8,128)(2,1)} %wc_h.1, bf16[8,128,128]{2,1,0:T(8,128)(2,1)} %wd_h.1, bf16[4,64,128]{2,1,0:T(8,128)(2,1)} %bitcast.8, ...), custom_call_target="tpu_custom_call" | custom-call | tf_op jit(solution)/shard_map/pallas_call | solution.py:741
  54.9 1.6 %shard_map.112 = (bf16[4,64,128]{2,1,0:T(8,128)(2,1)}, bf16[4,512,128]{2,1,0:T(8,128)(2,1)}, f32[3,3,3,128,128]{4,3,2,1,0:T(8,128)}, f32[8,128,128]{2,1,0:T(8,128)}) custom-call(bf16[3,12,128,128]{3,2,1,0:T(8,128)(2,1)S(1)} %bitcast.6, bf16[4,64,128]{2,1,0:T(8,128)(2,1)S(1)} %get-tuple-element.12.pooled, bf16[4,512,128]{2,1,0:T(8,128)(2,1)S(1)} %get-tuple-element.13.dfeats), custom_call_target="tpu_custom_call" | custom-call | tf_op jit(solution)/shard_map/pallas_call | solution.py:774

commit v6 on v5

--- a/solution.py
+++ b/solution.py
@@ -155,7 +155,7 @@
             )
         )
     ]
-    for one in loads:
+    for one in loads[:3]:
         one.start()
 
     barrier = pltpu.get_barrier_semaphore()
@@ -249,6 +249,8 @@
         one.start()
     sent.extend(copies)
 
+    for one in loads[3:]:
+        one.start()
     loads[3].wait()
 
     def x_layer(s, chunk, halo):
@@ -579,6 +581,8 @@
     for part in range(3):
         grad_conv(part, (3,), True)
         core_send(part)
+        if part > 0:
+            scatter_send(part - 1)
 
     inner_faces(bg, lambda side: [(8 - 7 * side) * 10 + z for z in range(1, 9)], ogyi, rgyi)
     copies_y = halo_send(8, 1, lambda side, b: ogyi[side, b], sgyi, rgyi)
@@ -600,8 +604,7 @@
                 rgxi[5 + b, side, rows] = face
     copies_x = halo_send(9, 0, lambda side, b: ogxi[side, b], sgxi, rgxi)
 
-    for part in range(3):
-        scatter_send(part)
+    scatter_send(2)
 
     halo = halo_recv(2, copies, rgz)
     ends = [

time: 56.6 us -> 56.8 us (level)
  no operation moved by 1% of the time
where the time goes in v6:
time: 56.8 us; the launch traced here: 56.7 us
  Pallas kernels  56.1 us (99%)
  between operations  0.64 us (1%)
    pallas_call x1, Pallas kernels, per_device(): pl.pallas_call(kernel, out_shape=(pltpu.VMEM((4, 64, 128), BF), pltpu.VME...  54.5 us
    pallas_call x1, Pallas kernels, per_device(): pl.pallas_call(functools.partial(epilogue, norm), out_shape=(jax.ShapeDty...  1.62 us

profile of v6, /device:TPU:1, one launch (start us, length us, event | category | flops | bytes accessed | tf_op | source)
XLA Modules:
  0.0 56.7 jit_solution(13332898998207249895)
XLA Ops:
  0.6 54.5 %shard_map.111 = (bf16[4,64,128]{2,1,0:T(8,128)(2,1)S(1)}, bf16[4,512,128]{2,1,0:T(8,128)(2,1)S(1)}, bf16[3,2,48,16,128]{4,3,2,1,0:T(8,128)(2,1)S(1)}) custom-call(bf16[4,512,128]{2,1,0:T(8,128)(2,1)} %bitcast.7, bf16[27,128,128]{2,1,0:T(8,128)(2,1)} %wc_h.1, bf16[8,128,128]{2,1,0:T(8,128)(2,1)} %wd_h.1, bf16[4,64,128]{2,1,0:T(8,128)(2,1)} %bitcast.8, ...), custom_call_target="tpu_custom_call" | custom-call | tf_op jit(solution)/shard_map/pallas_call | solution.py:744
  55.1 1.6 %shard_map.112 = (bf16[4,64,128]{2,1,0:T(8,128)(2,1)}, bf16[4,512,128]{2,1,0:T(8,128)(2,1)}, f32[3,3,3,128,128]{4,3,2,1,0:T(8,128)}, f32[8,128,128]{2,1,0:T(8,128)}) custom-call(bf16[3,12,128,128]{3,2,1,0:T(8,128)(2,1)S(1)} %bitcast.6, bf16[4,64,128]{2,1,0:T(8,128)(2,1)S(1)} %get-tuple-element.12.pooled, bf16[4,512,128]{2,1,0:T(8,128)(2,1)S(1)} %get-tuple-element.13.dfeats), custom_call_target="tpu_custom_call" | custom-call | tf_op jit(solution)/shard_map/pallas_call | solution.py:777
